TPU v7x, 128 devices: a whole 4x4x4 slice. The times are simulated.
128 devices in a mesh: dp: 32 (over z, y, core), segment: 4 (over x).
Axes of the slice: x: 4, y: 4, z: 4, core: 2. Of those that a mesh axis runs over, the one named last changes fastest.
Arguments:
- patches: bfloat16 [4, 512, 64, 588], P('segment', 'dp'), may hold values from -6 to 6
- image_shape: int32 [4, 512, 2], P('segment', 'dp'), may hold values from 6 to 8
- keep_list: int32 [4, 512, 32], P('segment', 'dp'), may hold values from 0 to 63, as said below
- kept_count: int32 [4, 512], P('segment', 'dp'), may hold values from 16 to 32
- dest_seq: int32 [4, 512], P('segment', 'dp'), may hold values from 0 to 31, as said below
- embed_weight: bfloat16 [588, 6144], replicated, may hold values from -0.25 to 0.25
- pos_rows: bfloat16 [8, 6144], replicated, may hold values from -3 to 3
- pos_cols: bfloat16 [8, 6144], replicated, may hold values from -3 to 3
- ln_gain: bfloat16 [4, 6144], P('segment'), may hold values from 0.099609375 to 1.8984375
- qkv_weight: bfloat16 [4, 6144, 384], P('segment'), may hold values from -10 to 10
- norm_gains: float32 [4, 2, 128], P('segment'), may hold values from 0.5 to 4
- out_weight: bfloat16 [4, 128, 6144], P('segment'), may hold values from -0.5 to 0.5
Outputs:
- handed: bfloat16 [4, 16384, 6144], P('segment', 'dp')
Inputs may be any that keep to these rules, and one draw needn't show every extreme that they name: `dest_seq`: each device's 16 images go to 16 sequences' worth of slots: every sequence receives exactly 16 images, at most 1 from one device; the kept patches from one device to one sequence number at most 32 and those of one sequence at most 512, both reached in every micro-batch. `keep_list`: entries of one image are distinct and below its height times width.
All inputs are finite; a program needn't handle non-finite values.
Results may differ from a plain program's by a relative error of at most 0.023.
The roundings to bfloat16 on the way count: a program that leaves them out, or rounds other values in their place, can miss the bound.
Values may be sent and summed in bfloat16 or wider, within the bound.
No kernel may reach another device: no remote copies, remote signals or barrier semaphores. Data moves between devices by JAX's collectives and lax.ppermute only.
A program may use at most 128 MiB of HBM per device.

v0:
```python
import math

import jax
import jax.numpy as jnp
from jax import lax
from jax.sharding import PartitionSpec as P

eps = 1e-06


def prefix(value, axis, join, neutral):
    count, mine = (lax.axis_size(axis), lax.axis_index(axis))
    pieces = lax.all_gather(value, axis)
    running = jnp.full_like(value, 0) + jnp.asarray(neutral, value.dtype)

    def lap(position, running):
        longer = join(running, pieces[position])
        return jnp.where(position < mine, longer, running)

    return lax.fori_loop(0, count - 1, lap, running)


def shifted(value, axis, steps):
    count = lax.axis_size(axis)
    pairs = [(source, (source + steps) % count) for source in range(count)]
    return lax.ppermute(value, axis, pairs)


def embed_rows(raw_rows, row_index, col_index, embed_weight, pos_rows, pos_cols):
    levels = jnp.arange(pos_rows.shape[0], dtype=jnp.int32)
    row_hot = (row_index[:, None] == levels[None, :]).astype(jnp.bfloat16)
    col_hot = (col_index[:, None] == levels[None, :]).astype(jnp.bfloat16)
    total = jnp.dot(raw_rows, embed_weight, preferred_element_type=jnp.float32)
    total = total + jnp.dot(row_hot, pos_rows, preferred_element_type=jnp.float32)
    return total + jnp.dot(col_hot, pos_cols, preferred_element_type=jnp.float32)


def head_norm(values, gain):
    centre = values - jnp.mean(values, axis=-1, keepdims=True)
    spread = jnp.mean(centre * centre, axis=-1, keepdims=True)
    return (centre * lax.rsqrt(spread + eps) * gain).astype(jnp.bfloat16)


def attend(queries, keys, values, query_ids, key_ids):
    head_dim = queries.shape[2]
    scores = jnp.einsum(
        "qhd,khd->hqk", queries, keys, preferred_element_type=jnp.float32
    ) / math.sqrt(head_dim)
    allowed = query_ids[:, None] == key_ids[None, :]
    scores = jnp.where(allowed[None], scores, -jnp.inf)
    top = jnp.max(scores, axis=-1, keepdims=True)
    expo = jnp.exp(scores - top)
    weights = (expo / jnp.sum(expo, axis=-1, keepdims=True)).astype(jnp.bfloat16)
    return jnp.einsum("hqk,khd->qhd", weights, values, preferred_element_type=jnp.float32).astype(
        jnp.bfloat16
    )


def section_layer(tokens, seq_ids, ln_gain, qkv_weight, norm_gains, out_weight):
    seq_len = tokens.shape[0]
    head_dim = norm_gains.shape[1]
    width = out_weight.shape[0]
    heads = width // head_dim
    floats = tokens.astype(jnp.float32)
    centre = floats - jnp.mean(floats, axis=1, keepdims=True)
    spread = jnp.mean(centre * centre, axis=1, keepdims=True)
    normed = (centre * lax.rsqrt(spread + eps) * ln_gain.astype(jnp.float32)).astype(jnp.bfloat16)
    mixed = jnp.dot(normed, qkv_weight, preferred_element_type=jnp.float32)
    queries = head_norm(mixed[:, :width].reshape(seq_len, heads, head_dim), norm_gains[0])
    keys = head_norm(mixed[:, width : 2 * width].reshape(seq_len, heads, head_dim), norm_gains[1])
    values = mixed[:, 2 * width :].reshape(seq_len, heads, head_dim).astype(jnp.bfloat16)
    attended = attend(queries, keys, values, seq_ids, seq_ids)
    attended = attended.reshape(seq_len, width)
    result = floats + jnp.dot(attended, out_weight, preferred_element_type=jnp.float32)
    return jnp.where((seq_ids >= 0)[:, None], result, 0.0).astype(jnp.bfloat16)


def shards(
    patches,
    image_shape,
    keep_list,
    kept_count,
    dest_seq,
    embed_weight,
    pos_rows,
    pos_cols,
    ln_gain,
    qkv_weight,
    norm_gains,
    out_weight,
):
    groups = lax.axis_size("dp")
    device = lax.axis_index("dp")
    images = patches.shape[1]
    kept_max = keep_list.shape[2]
    seq_len = images * kept_max
    capacity = max(1, images // groups) * kept_max
    model_width = embed_weight.shape[1]
    patch_width = embed_weight.shape[0]
    counts = kept_count[0]
    targets = dest_seq[0]
    seq_range = jnp.arange(groups, dtype=jnp.int32)
    target_hot = (targets[:, None] == seq_range[None, :]).astype(jnp.int32)
    sent = jnp.sum(target_hot * counts[:, None], axis=0)
    base = prefix(sent, "dp", lambda first, second: first + second, jnp.zeros_like(sent))
    order = jnp.arange(images, dtype=jnp.int32)
    earlier = (order[None, :] < order[:, None]) & (targets[None, :] == targets[:, None])
    within = jnp.sum(jnp.where(earlier, counts[None, :], 0), axis=1)
    start = jnp.sum(target_hot * base[None, :], axis=1).astype(jnp.int32) + within
    offsets = jnp.arange(kept_max, dtype=jnp.int32)
    live = offsets[None, :] < counts[:, None]
    slot = jnp.where(
        live, targets[:, None] * capacity + within[:, None] + offsets[None, :], groups * capacity
    ).reshape(-1)
    position = (start[:, None] + offsets[None, :]).reshape(-1)
    image_ids = jnp.broadcast_to((device * images + order)[:, None], (images, kept_max)).reshape(-1)
    picks = keep_list[0]
    widths = image_shape[0][:, 1]
    row_index = (picks // widths[:, None]).reshape(-1)
    col_index = (picks % widths[:, None]).reshape(-1)
    raw = jnp.take_along_axis(patches[0], picks[:, :, None], axis=1).reshape(-1, patch_width)
    buffer_len = groups * capacity
    slot_target = jnp.full((buffer_len,), seq_len, jnp.int32).at[slot].set(position, mode="drop")
    slot_ids = jnp.full((buffer_len,), -1, jnp.int32).at[slot].set(image_ids, mode="drop")
    embedded = embed_rows(raw, row_index, col_index, embed_weight, pos_rows, pos_cols).astype(
        jnp.bfloat16
    )
    row_buffer = (
        jnp.zeros((buffer_len, model_width), jnp.bfloat16).at[slot].set(embedded, mode="drop")
    )
    rows_in, target_in, ids_in = (
        lax.all_to_all(
            row_buffer.reshape(groups, capacity, model_width),
            "dp",
            split_axis=0,
            concat_axis=0,
            tiled=True,
        ),
        lax.all_to_all(
            slot_target.reshape(groups, capacity), "dp", split_axis=0, concat_axis=0, tiled=True
        ),
        lax.all_to_all(
            slot_ids.reshape(groups, capacity), "dp", split_axis=0, concat_axis=0, tiled=True
        ),
    )
    target_flat = target_in.reshape(-1)
    tokens = (
        jnp.zeros((seq_len, model_width), jnp.bfloat16)
        .at[target_flat]
        .set(rows_in.reshape(-1, model_width), mode="drop")
    )
    seq_ids = (
        jnp.full((seq_len,), -1, jnp.int32).at[target_flat].set(ids_in.reshape(-1), mode="drop")
    )
    section = section_layer(
        tokens, seq_ids, ln_gain[0], qkv_weight[0], norm_gains[0], out_weight[0]
    )
    return shifted(section[None], "segment", 1)


def solution(mesh):
    return jax.shard_map(
        shards,
        mesh=mesh,
        in_specs=(
            P("segment", "dp", None, None),
            P("segment", "dp", None),
            P("segment", "dp", None),
            P("segment", "dp"),
            P("segment", "dp"),
            P(),
            P(),
            P(),
            P("segment", None),
            P("segment", None, None),
            P("segment", None, None),
            P("segment", None, None),
        ),
        out_specs=P("segment", "dp", None),
        check_vma=False,
    )
```

profile of v0, /device:TPU:48, one launch (start us, length us, event | category | flops | bytes accessed | tf_op | source)
XLA Modules:
  0.0 447.6 jit_solution(3330833553242852620)
XLA Ops:
  1.8 1.3 dynamic-slice
  4.1 13.5 %all-reduce = s32[1024]{0:T(1024)S(1)} all-reduce(s32[1024]{0:T(1024)S(1)} %dynamic-update-slice), channel_id=2, replica_groups=mesh['dp'=32,'segment'=4] {'dp'}, use_global_device_ids=true, to_apply=%add | all-reduce | flops 1024 | bytes 8192
  17.7 1.2 while.14
  21.3 2.4 scatter_custom_fusion
  24.5 8.7 %all-to-all-start = ((s32[32,1,32]{2,1,0:T(1,128)}), s32[32,1,32]{2,1,0:T(1,128)}, u32[]{:S(2)}, u32[]{:S(2)}) async-start(s32[32,1,32]{2,1,0:T(1,128)} %all_to_all.15), calls=%async_computation | async-start | bytes 32768 | tf_op jit(solution)/shard_map/all_to_all | solution.py:139
  36.9 7.2 %fusion.30 = f32[512,6144]{1,0:T(8,128)} fusion(bf16[8,6144]{1,0:T(8,128)(2,1)} %param.20, s32[512]{0:T(512)S(1)} %get-tuple-element.113), kind=kOutput, calls=%fused_computation.50 | convolution fusion | flops 50335744 | bytes 12683264 | tf_op jit(solution)/shard_map/dot_general | solution.py:34
  44.1 4.3 gather_fusion
  48.3 11.2 %fusion.22 = f32[512,6144]{1,0:T(8,128)} fusion(bf16[588,6144]{1,0:T(8,128)(2,1)} %param.19, bf16[512,588]{1,0:T(8,128)(2,1)S(1)} %gather_fusion, pred[512]{0:T(512)(128)(4,1)S(1)} %compare_and_fusion), kind=kOutput, calls=%fused_computation.37 | convolution fusion | flops 3699677184 | bytes 20410880 | tf_op jit(solution)/shard_map/dot_general | solution.py:33
  59.7 2.4 scatter_custom_fusion.1
  62.8 7.7 %all-to-all-start.1 = ((s32[32,1,32]{2,1,0:T(1,128)}), s32[32,1,32]{2,1,0:T(1,128)S(1)}, u32[]{:S(2)}, u32[]{:S(2)}) async-start(s32[32,1,32]{2,1,0:T(1,128)} %all_to_all.17), calls=%async_computation.1 | async-start | bytes 32768 | tf_op jit(solution)/shard_map/all_to_all | solution.py:142
  70.6 12.0 %add_convert_fusion = bf16[512,6144]{1,0:T(8,128)(2,1)} fusion(f32[512,6144]{1,0:T(8,128)} %fusion.22, f32[512,6144]{1,0:T(8,128)} %fusion.30, bf16[8,6144]{1,0:T(8,128)(2,1)S(1)} %copy-done.4, s32[512]{0:T(512)S(1)} %get-tuple-element.112), kind=kOutput, calls=%fused_computation.18 | convolution fusion | flops 59772928 | bytes 31557632 | tf_op jit(solution)/shard_map/dot_general | solution.py:35
  82.6 18.0 %scatter_custom_fusion.3 = bf16[1024,6144]{1,0:T(8,128)(2,1)} fusion(s32[512]{0:T(512)S(1)} %bitcast.60, bf16[512,6144]{1,0:T(8,128)(2,1)} %add_convert_fusion, bf16[]{:T(256)} %constant.84.clone.1), kind=kCustom, calls=%fused_computation.24 | custom fusion | bytes 12583424 | tf_op jit(solution)/shard_map/scatter | solution.py:129
  100.6 7.6 %all-to-all-start.2 = ((bf16[32,32,6144]{2,1,0:T(8,128)(2,1)}), bf16[32,32,6144]{2,1,0:T(8,128)(2,1)}, u32[]{:S(2)}, u32[]{:S(2)}) async-start(bf16[32,32,6144]{2,1,0:T(8,128)(2,1)} %bitcast.50), calls=%async_computation.2 | async-start | bytes 25165824 | tf_op jit(solution)/shard_map/all_to_all | solution.py:132
  108.7 1.4 reduce.18
  111.0 4.3 scatter_custom_fusion.2
  115.3 148.1 %all-to-all-done.2 = bf16[32,32,6144]{2,1,0:T(8,128)(2,1)} async-done(((bf16[32,32,6144]{2,1,0:T(8,128)(2,1)}), bf16[32,32,6144]{2,1,0:T(8,128)(2,1)}, u32[]{:S(2)}, u32[]{:S(2)}) %all-to-all-start.2) | async-done | bytes 12582944 | tf_op jit(solution)/shard_map/all_to_all | solution.py:132
  263.4 22.6 %scatter_custom_fusion.4 = bf16[512,6144]{1,0:T(8,128)(2,1)} fusion(s32[1024]{0:T(1024)S(1)} %bitcast.57, bf16[1024,6144]{1,0:T(8,128)(2,1)} %bitcast.13, bf16[]{:T(256)} %constant.84.clone.1), kind=kCustom, calls=%fused_computation.27 | custom fusion | bytes 6291968 | tf_op jit(solution)/shard_map/scatter | solution.py:150
  286.1 3.8 convert_reduce_fusion
  290.6 1.8 fusion.2
  292.4 5.6 %fusion.8 = f32[512,384]{0,1:T(8,128)S(1)} fusion(bf16[512,6144]{1,0:T(8,128)(2,1)S(1)} %copy-done.1, f32[6144]{0:T(1024)S(1)} %bitcast.52, f32[512]{0:T(512)S(1)} %add_rsqrt_fusion.2, f32[512]{0:T(512)S(1)} %broadcast_multiply_fusion.2, bf16[1,6144,384]{2,1,0:T(8,128)(2,1)} %param.23), kind=kOutput, calls=%fused_computation.20 | convolution fusion | flops 2431647744 | bytes 11825152 | tf_op jit(solution)/shard_map/dot_general | solution.py:68
  299.8 6.5 %fusion.7 = bf16[1,512,6144]{2,1,0:T(8,128)(2,1)} fusion(bf16[512,6144]{1,0:T(8,128)(2,1)} %scatter_custom_fusion.4, pred[512]{0:T(512)(128)(4,1)S(1)} %broadcast_compare_fusion, bf16[1,128,6144]{2,1,0:T(8,128)(2,1)S(1)} %copy-done, f32[512,512]{0,1:T(8,128)} %copy-done.3, f32[512]{0:T(512)S(1)} %fusion.21, f32[512]{0:T(512)S(1)} %get-tuple-element.121, ...), kind=kOutput, calls=%fused_computation.19 | convolution fusion | flops 885850112 | bytes 15340032 | tf_op jit(solution)/shard_map/dot_general | solution.py:74
  306.3 1.5 collective-permute-start
  307.8 137.0 %collective-permute-done = bf16[1,512,6144]{2,1,0:T(8,128)(2,1)S(1)} collective-permute-done((bf16[1,512,6144]{2,1,0:T(8,128)(2,1)}, bf16[1,512,6144]{2,1,0:T(8,128)(2,1)S(1)}, u32[]{:S(2)}, u32[]{:S(2)}) %collective-permute-start) | collective-permute-done | bytes 6291488 | tf_op jit(solution)/shard_map/ppermute | solution.py:26
  444.7 2.7 copy.21
  (97 shorter events, 14.2 us)
Async XLA Ops:
  0.0 299.8 %copy-start = (bf16[1,128,6144]{2,1,0:T(8,128)(2,1)S(1)}, bf16[1,128,6144]{2,1,0:T(8,128)(2,1)}, u32[]{:S(2)}) copy-start(bf16[1,128,6144]{2,1,0:T(8,128)(2,1)} %param.25) | copy-start | bytes 4718596
  0.0 44.1 %copy-start.2 = (bf16[1,16,64,588]{3,2,1,0:T(8,128)(2,1)S(1)}, bf16[1,16,64,588]{3,2,1,0:T(8,128)(2,1)}, u32[]{:S(2)}) copy-start(bf16[1,16,64,588]{3,2,1,0:T(8,128)(2,1)} %param.14) | copy-start | bytes 3612676
  24.5 38.4 %all-to-all-start = ((s32[32,1,32]{2,1,0:T(1,128)}), s32[32,1,32]{2,1,0:T(1,128)}, u32[]{:S(2)}, u32[]{:S(2)}) async-start(s32[32,1,32]{2,1,0:T(1,128)} %all_to_all.15), calls=%async_computation | async-start | bytes 32768 | tf_op jit(solution)/shard_map/all_to_all | solution.py:139
  48.3 22.2 %copy-start.4 = (bf16[8,6144]{1,0:T(8,128)(2,1)S(1)}, bf16[8,6144]{1,0:T(8,128)(2,1)}, u32[]{:S(2)}) copy-start(bf16[8,6144]{1,0:T(8,128)(2,1)} %param.21) | copy-start | bytes 294916
  62.8 37.7 %all-to-all-start.1 = ((s32[32,1,32]{2,1,0:T(1,128)}), s32[32,1,32]{2,1,0:T(1,128)S(1)}, u32[]{:S(2)}, u32[]{:S(2)}) async-start(s32[32,1,32]{2,1,0:T(1,128)} %all_to_all.17), calls=%async_computation.1 | async-start | bytes 32768 | tf_op jit(solution)/shard_map/all_to_all | solution.py:142
  100.6 7.6 %copy-start.5 = (bf16[1,6144]{1,0:T(2,128)(2,1)S(1)}, bf16[1,6144]{1,0:T(2,128)(2,1)}, u32[]{:S(2)}) copy-start(bf16[1,6144]{1,0:T(2,128)(2,1)} %param.22) | copy-start | bytes 36868
  100.6 7.6 %copy-start.6 = (f32[1,2,128]{2,1,0:T(2,128)S(1)}, f32[1,2,128]{2,1,0:T(2,128)}, u32[]{:S(2)}) copy-start(f32[1,2,128]{2,1,0:T(2,128)} %param.24) | copy-start | bytes 3076
  100.6 162.9 %all-to-all-start.2 = ((bf16[32,32,6144]{2,1,0:T(8,128)(2,1)}), bf16[32,32,6144]{2,1,0:T(8,128)(2,1)}, u32[]{:S(2)}, u32[]{:S(2)}) async-start(bf16[32,32,6144]{2,1,0:T(8,128)(2,1)} %bitcast.50), calls=%async_computation.2 | async-start | bytes 25165824 | tf_op jit(solution)/shard_map/all_to_all | solution.py:132
  286.0 4.6 %copy-start.1 = (bf16[512,6144]{1,0:T(8,128)(2,1)S(1)}, bf16[512,6144]{1,0:T(8,128)(2,1)}, u32[]{:S(2)}) copy-start(bf16[512,6144]{1,0:T(8,128)(2,1)} %scatter_custom_fusion.4) | copy-start | bytes 18874372
  298.6 1.0 copy-start.3
  306.3 138.5 %collective-permute-start = (bf16[1,512,6144]{2,1,0:T(8,128)(2,1)}, bf16[1,512,6144]{2,1,0:T(8,128)(2,1)S(1)}, u32[]{:S(2)}, u32[]{:S(2)}) collective-permute-start(bf16[1,512,6144]{2,1,0:T(8,128)(2,1)} %fusion.7), channel_id=1, source_target_pairs={{0,1},{1,2},{2,3},{3,0},{4,5},{5,6},{6,7},{7,4},{8,9},{9,10},{10,1... | collective-permute-start | bytes 18874376 | tf_op jit(solution)/shard_map/ppermute | solution.py:26
where the time goes:
time: 455 us; the launch traced here: 448 us
  waiting for transfers between devices  285 us (63%)
  local copies, waits for them, and re-layouts  63.9 us (14%)
  matrix products  42.9 us (9%)
  starting transfers between devices  25.5 us (6%)
  other arithmetic  14.9 us (3%)
  blocking collectives  13.5 us (3%)
    all_to_all x1, waiting for transfers between devices, shards(): lax.all_to_all(row_buffer.reshape(groups, capacity, model_width), 'dp', s...  148 us
    ppermute x1, waiting for transfers between devices, shifted(): return lax.ppermute(value, axis, pairs)  137 us
    scatter x1, local copies, waits for them, and re-layouts, shards(): tokens = jnp.zeros((seq_len, model_width), jnp.bfloat16).at[target_flat]....  22.6 us
    scatter x1, local copies, waits for them, and re-layouts, shards(): jnp.zeros((buffer_len, model_width), jnp.bfloat16).at[slot]  18 us
    unnamed x1, blocking collectives  13.5 us
    dot_general x1, matrix products, embed_rows(): jnp.dot(col_hot, pos_cols, preferred_element_type=jnp.float32)  12 us
    dot_general x1, matrix products, embed_rows(): total = jnp.dot(raw_rows, embed_weight, preferred_element_type=jnp.float32)  11.2 us
  transfers between devices with their start and end apart: 4, of which 2 were waited for; matrix products, arithmetic and copies ran while one was open for 15% of the time, Pallas kernels for 0%

commit v1 on v0

v1 whole, which is shorter than its diff:
```python
import math

import jax
import jax.numpy as jnp
from jax import lax
from jax.experimental import pallas as pl
from jax.experimental.pallas import tpu as pltpu
from jax.sharding import PartitionSpec as P

eps = 1e-06
LANES = 640
TAIL = 512
ROW_AT = 588 - TAIL
COL_AT = 596 - TAIL
SRC_AT = 604 - TAIL
SRC_END = 636 - TAIL
TILE = 1024
EARLY = 2
STORE = 20480
MIB = 1 << 20


def iota(shape, axis):
    return lax.broadcasted_iota(jnp.int32, shape, axis)


def dot(a, b, dims=((1,), (0,))):
    return lax.dot_general(a, b, (dims, ((), ())), preferred_element_type=jnp.float32)


def as_bf16(mask):
    return mask.astype(jnp.float32).astype(jnp.bfloat16)


def pack_kernel(
    shape_hbm, count_hbm, dest_hbm, keep_hbm, patches_hbm, weight_hbm, out_ref, half_ref, token_ref,
    shape, count, dest, keep, patches, sems, patch_sems,
):
    images, patch_max, _ = patches.shape
    kept_max = keep.shape[1]
    parts = patch_sems.shape[0]
    step = images // parts
    small = [
        pltpu.make_async_copy(source, target, sems.at[n])
        for n, (source, target) in enumerate(
            ((shape_hbm, shape), (count_hbm, count), (dest_hbm, dest), (keep_hbm, keep))
        )
    ]
    large = [
        pltpu.make_async_copy(
            patches_hbm.at[pl.ds(n * step, step)], patches.at[pl.ds(n * step, step)], patch_sems.at[n]
        )
        for n in range(parts)
    ]
    for copy in small + large:
        copy.start()
    device = lax.axis_index("dp")
    share = half_ref.shape[0]
    half = pltpu.make_async_copy(
        weight_hbm.at[pl.ds(pl.multiple_of(device % 2 * share, share), share)], half_ref, sems.at[4]
    )
    half.start()
    out_ref[...] = jnp.zeros_like(out_ref)
    token_ref[...] = jnp.zeros_like(token_ref)
    number = iota((patch_max, 128), 0)
    lane = iota((patch_max, 128), 1)
    source = lane == SRC_AT + device
    for copy in small:
        copy.wait()
    for g in range(images):
        if g % step == 0:
            large[g // step].wait()
        width = shape[1, g]
        row = jnp.zeros_like(number)
        for k in range(1, 8):
            row = row + (number >= k * width).astype(jnp.int32)
        col = number - row * width
        flags = as_bf16((lane == ROW_AT + row) | (lane == COL_AT + col) | source)
        picked = (iota((patch_max, kept_max), 0) == keep[g : g + 1, :]) & (
            iota((patch_max, kept_max), 1) < count[0, g]
        )
        picked = as_bf16(picked)
        there = dest[0, g]
        body = dot(picked, patches[g, :, :TAIL], ((0,), (0,)))
        out_ref[there, :, :TAIL] = body.astype(jnp.bfloat16)
        last = jnp.concatenate([patches[g, :, TAIL:], flags[:, ROW_AT:]], axis=1)
        out_ref[there, :, TAIL:] = dot(picked, last, ((0,), (0,))).astype(jnp.bfloat16)
    half.wait()


def compact_kernel(weights_hbm, recv_ref, out_ref, early_ref, sems):
    copies = tile_copies(weights_hbm, 0, early_ref, sems)
    for copy in copies:
        copy.start()
    sources, kept_max, lanes = recv_ref.shape
    total = sources * kept_max
    blocks = total // 128
    seq_len = out_ref.shape[0]
    received = recv_ref[...].reshape(total, lanes)
    at = iota((8, 128), 1)
    select = as_bf16((at >= SRC_AT) & (at < SRC_END))
    live = dot(select, received[:, TAIL:], ((1,), (1,)))
    group = iota((8, 128), 0)
    packed = jnp.zeros((8, 128), jnp.float32)
    for b in range(blocks):
        packed = jnp.where(group == b, live[:, b * 128 : (b + 1) * 128], packed)
    before = as_bf16(iota((128, 128), 0) < iota((128, 128), 1))
    within = dot(packed.astype(jnp.bfloat16), before)
    sums = jnp.sum(packed, axis=1, keepdims=True)
    base = jnp.zeros((8, 1), jnp.float32)
    for b in range(blocks - 1):
        base = base + jnp.where(iota((8, 1), 0) > b, sums[b : b + 1, :], 0.0)
    place = jnp.where(packed > 0.5, within + base, -1.0).astype(jnp.int32)
    slot = iota((seq_len, 128), 0)
    hot = jnp.concatenate([as_bf16(slot == place[b : b + 1, :]) for b in range(blocks)], axis=1)
    out_ref[...] = dot(hot, received).astype(jnp.bfloat16)
    for copy in copies:
        copy.wait()


def lane_sums(values, sums):
    for at in range(0, values.shape[1], 128):
        sums = sums + values[:, at : at + 128]
    return sums


def head_norm(values, gain):
    centre = values - jnp.mean(values, axis=-1, keepdims=True)
    spread = jnp.mean(centre * centre, axis=-1, keepdims=True)
    return (centre * lax.rsqrt(spread + eps) * gain).astype(jnp.bfloat16)


def weight_kernel(token_hbm, embed_hbm, tail_hbm, qkv_hbm, out_hbm, embed, qkv, sems, out_sems):
    tiles, lanes, _ = embed.shape
    depth = lanes - tail_hbm.shape[0]
    copies, results = [], []
    for t in range(tiles):
        columns = pl.ds(t * TILE, TILE)
        copies.append(
            (
                pltpu.make_async_copy(
                    embed_hbm.at[pl.ds(0, depth), columns], embed.at[t, pl.ds(0, depth)], sems.at[2 * t]
                ),
                pltpu.make_async_copy(
                    tail_hbm.at[:, columns],
                    embed.at[t, pl.ds(depth, tail_hbm.shape[0])],
                    sems.at[2 * t + 1],
                ),
            )
        )
        results.append(
            pltpu.make_async_copy(embed.at[t], out_hbm.at[pl.ds(t * lanes, lanes)], out_sems.at[t])
        )
    copies.append((pltpu.make_async_copy(qkv_hbm, qkv, sems.at[2 * tiles]),))
    results.append(pltpu.make_async_copy(qkv, qkv_part(out_hbm, tiles * lanes, qkv), out_sems.at[tiles]))
    for pair in copies:
        for copy in pair:
            copy.start()
    for pair, result in zip(copies, results):
        for copy in pair:
            copy.wait()
        result.start()
    for result in results:
        result.wait()


def qkv_part(weights, first, qkv):
    return weights.at[pl.ds(first, qkv.shape[0]), pl.ds(0, qkv.shape[1])]


def tile_copies(weights_hbm, first, embed, sems):
    tiles, lanes, _ = embed.shape
    return [
        pltpu.make_async_copy(weights_hbm.at[pl.ds((first + t) * lanes, lanes)], embed.at[t], sems.at[t])
        for t in range(tiles)
    ]


def attend_kernel(
    x_ref, gain_ref, norm_ref, early_ref, weights_hbm, half_hbm,
    out_ref, late_ref, same_half_hbm, tokens, qkv, sems, qkv_sem,
):
    early, late = early_ref.shape[0], late_ref.shape[0]
    copies = tile_copies(weights_hbm, early, late_ref, sems)
    for copy in copies:
        copy.start()
    lanes = late_ref.shape[1]
    qkv_copy = pltpu.make_async_copy(
        qkv_part(weights_hbm, (early + late) * lanes, qkv), qkv, qkv_sem.at[0]
    )
    width = (early + late) * TILE
    x = x_ref[...]
    rows = x.shape[0]
    spans = [slice(at, at + TILE) for at in range(0, width, TILE)]
    total = jnp.zeros((rows, 128), jnp.float32)
    squares = jnp.zeros((rows, 128), jnp.float32)
    for t, span in enumerate(spans):
        if t == early:
            copies[0].wait()
            copies[1].wait()
            qkv_copy.start()
        if t == early + 2:
            for copy in copies[2:]:
                copy.wait()
        tile = early_ref[t] if t < early else late_ref[t - early]
        part = dot(x, tile).astype(jnp.bfloat16)
        tokens[:, span] = part
        part = part.astype(jnp.float32)
        total = lane_sums(part, total)
        squares = lane_sums(part * part, squares)
    mean = jnp.sum(total, axis=1, keepdims=True) / width
    squares = jnp.sum(squares, axis=1, keepdims=True) / width
    scale = lax.rsqrt(jnp.maximum(squares - mean * mean, 0.0) + eps)
    qkv_copy.wait()
    mixed = jnp.zeros((rows, qkv.shape[1]), jnp.float32)
    for span in spans:
        centre = tokens[:, span].astype(jnp.float32) - mean
        normed = (centre * scale * gain_ref[:, span].astype(jnp.float32)).astype(jnp.bfloat16)
        mixed = mixed + dot(normed, qkv[span, :])
    head = norm_ref.shape[1]
    queries = head_norm(mixed[:, :head], norm_ref[0:1, :])
    keys = head_norm(mixed[:, head : 2 * head], norm_ref[1:2, :])
    values = mixed[:, 2 * head :].astype(jnp.bfloat16)
    lane = iota((rows, 128), 1)
    flags = x[:, TAIL:].astype(jnp.float32)
    flags = jnp.where((lane >= SRC_AT) & (lane < SRC_END), flags, 0.0)
    live = jnp.sum(flags, axis=1, keepdims=True) > 0.5
    flags = flags.astype(jnp.bfloat16)
    same = dot(flags, flags, ((1,), (1,))) > 0.5
    scores = dot(queries, keys, ((1,), (1,))) / math.sqrt(head)
    scores = jnp.where(same, scores, -1e30)
    expo = jnp.exp(scores - jnp.max(scores, axis=1, keepdims=True))
    weights = (expo / jnp.sum(expo, axis=1, keepdims=True)).astype(jnp.bfloat16)
    out_ref[...] = jnp.where(live, dot(weights, values), 0.0).astype(jnp.bfloat16)


def embed_kernel(x_ref, early_ref, late_ref, out_ref):
    early, late = early_ref.shape[0], late_ref.shape[0]
    for t in range(early + late):
        tile = early_ref[t] if t < early else late_ref[t - early]
        out_ref[:, t * TILE : (t + 1) * TILE] = dot(x_ref[...], tile).astype(jnp.bfloat16)


def section_kernel(
    tokens_ref, attended_ref, mine_ref, other_ref, out_hbm, weight, out, sems
):
    half = mine_ref.shape[0]
    core = lax.axis_index("dp") % 2
    weight[pl.ds(pl.multiple_of(core * half, half), half), :] = mine_ref[...]
    weight[pl.ds(pl.multiple_of((1 - core) * half, half), half), :] = other_ref[...]
    results = []
    for t in range(out.shape[1] // TILE):
        span = slice(t * TILE, (t + 1) * TILE)
        part = tokens_ref[:, span].astype(jnp.float32)
        out[:, span] = (part + dot(attended_ref[...], weight[:, span])).astype(jnp.bfloat16)
        columns = pl.ds(t * TILE, TILE)
        result = pltpu.make_async_copy(out.at[:, columns], out_hbm.at[0, :, columns], sems.at[t])
        result.start()
        results.append(result)
    for result in results:
        result.wait()


VMEM = pl.BlockSpec(memory_space=pltpu.VMEM)
HBM = pl.BlockSpec(memory_space=pltpu.HBM)


def bf16(*shape):
    return jax.ShapeDtypeStruct(shape, jnp.bfloat16)


def call(kernel, out, in_specs, out_specs, scratch, limit, flops, aliases={}):
    return pl.pallas_call(
        kernel,
        out_shape=out,
        in_specs=in_specs,
        out_specs=out_specs,
        scratch_shapes=scratch,
        input_output_aliases=aliases,
        compiler_params=pltpu.CompilerParams(vmem_limit_bytes=limit * MIB),
        cost_estimate=pl.CostEstimate(flops=flops, bytes_accessed=MIB, transcendentals=0),
    )


def shards(
    patches,
    image_shape,
    keep_list,
    kept_count,
    dest_seq,
    embed_weight,
    pos_rows,
    pos_cols,
    ln_gain,
    qkv_weight,
    norm_gains,
    out_weight,
):
    groups = lax.axis_size("dp")
    segments = lax.axis_size("segment")
    images, patch_max, patch_width = patches.shape[1:]
    kept_max = keep_list.shape[2]
    seq_len = images * kept_max
    width = embed_weight.shape[1]
    head = out_weight.shape[1]
    tiles = width // TILE
    parts = 4
    onward = [(source, (source + 1) % segments) for source in range(segments)]
    pairs = [(source, source ^ 1) for source in range(groups)]
    dma = pltpu.SemaphoreType.DMA
    token = jax.ShapeDtypeStruct((8, 128), jnp.float32)

    packed, half, after_pack = call(
        pack_kernel,
        [bf16(groups, kept_max, LANES), bf16(head // 2, width), token],
        [HBM] * 6,
        [VMEM] * 3,
        [
            pltpu.SMEM((2, images), jnp.int32),
            pltpu.SMEM((1, images), jnp.int32),
            pltpu.SMEM((1, images), jnp.int32),
            pltpu.VMEM((images, kept_max), jnp.int32),
            pltpu.VMEM((images, patch_max, patch_width), jnp.bfloat16),
            dma((5,)),
            dma((parts,)),
        ],
        60,
        2 * images * kept_max * patch_max * LANES,
    )(image_shape[0].T, kept_count, dest_seq, keep_list[0], patches[0], out_weight[0])
    received = lax.all_to_all(packed, "dp", split_axis=0, concat_axis=0, tiled=True)

    half = lax.ppermute(half, "segment", onward)
    tail = jnp.concatenate(
        [
            embed_weight[LANES - 64 :],
            pos_rows,
            pos_cols,
            jnp.zeros((LANES - patch_width - 16, width), jnp.bfloat16),
        ],
        axis=0,
    )
    embed_scratch = pltpu.VMEM((tiles, LANES, TILE), jnp.bfloat16)
    qkv_scratch = pltpu.VMEM((width, 3 * head), jnp.bfloat16)
    weights = call(
        weight_kernel,
        bf16(STORE, TILE),
        [HBM] * 4,
        HBM,
        [embed_scratch, qkv_scratch, dma((2 * tiles + 1,)), dma((tiles + 1,))],
        20,
        MIB,
    )(after_pack, embed_weight, tail, qkv_weight[0])
    x, first_tiles = call(
        compact_kernel,
        [bf16(seq_len, LANES), bf16(EARLY, LANES, TILE)],
        [HBM, VMEM],
        [VMEM] * 2,
        [dma((EARLY,))],
        16,
        2 * seq_len * groups * kept_max * LANES,
    )(weights, received)
    next_x = lax.ppermute(x, "segment", onward)
    attended, other_tiles, half = call(
        attend_kernel,
        [bf16(seq_len, head), bf16(tiles - EARLY, LANES, TILE), bf16(head // 2, width)],
        [VMEM] * 4 + [HBM] * 2,
        [VMEM, VMEM, HBM],
        [
            pltpu.VMEM((seq_len, width), jnp.bfloat16),
            qkv_scratch,
            dma((tiles - EARLY,)),
            dma((1,)),
        ],
        34,
        2 * seq_len * width * (LANES + 3 * head),
        {5: 2},
    )(x, ln_gain, norm_gains[0], first_tiles, weights, half)
    next_attended = lax.ppermute(attended, "segment", onward)
    other = lax.ppermute(half, "dp", pairs)

    tokens = call(
        embed_kernel,
        bf16(seq_len, width),
        [VMEM] * 3,
        VMEM,
        [],
        16,
        2 * seq_len * width * LANES,
    )(next_x, first_tiles, other_tiles)
    return call(
        section_kernel,
        bf16(1, seq_len, width),
        [VMEM] * 4,
        HBM,
        [
            pltpu.VMEM((head, width), jnp.bfloat16),
            pltpu.VMEM((seq_len, width), jnp.bfloat16),
            dma((tiles,)),
        ],
        30,
        2 * seq_len * width * head,
    )(tokens, next_attended, half, other)


def solution(mesh):
    return jax.shard_map(
        shards,
        mesh=mesh,
        in_specs=(
            P("segment", "dp", None, None),
            P("segment", "dp", None),
            P("segment", "dp", None),
            P("segment", "dp"),
            P("segment", "dp"),
            P(),
            P(),
            P(),
            P("segment", None),
            P("segment", None, None),
            P("segment", None, None),
            P("segment", None, None),
        ),
        out_specs=P("segment", "dp", None),
        check_vma=False,
    )
```

time: 455 us -> 60.1 us (0.13)
  the two profiles are of different devices: /device:TPU:48 before, /device:TPU:1 now
where the time goes in v1:
time: 60.1 us; the launch traced here: 59.6 us
  Pallas kernels  31.6 us (53%)
  starting transfers between devices  16 us (27%)
  waiting for transfers between devices  5.99 us (10%)
  local copies, waits for them, and re-layouts  5.52 us (9%)
    pallas_call x1, Pallas kernels, shards(): call(attend_kernel, [bf16(seq_len, head), bf16(tiles - EARLY, LANES, TILE...  12 us
    all_to_all x1, starting transfers between devices, shards(): lax.all_to_all(packed, 'dp', split_axis=0, concat_axis=0, tiled=True)  9.75 us
    pallas_call x1, Pallas kernels, shards(): call(weight_kernel, bf16(STORE, TILE), [HBM] * 4, HBM, [embed_scratch, qk...  6.11 us
    all_to_all x1, waiting for transfers between devices, shards(): lax.all_to_all(packed, 'dp', split_axis=0, concat_axis=0, tiled=True)  5.98 us
    unnamed x16, local copies, waits for them, and re-layouts  5.43 us
    pallas_call x1, Pallas kernels, shards(): call(embed_kernel, bf16(seq_len, width), [VMEM] * 3, VMEM, [], 16, 2 * se...  5.05 us
    pallas_call x1, Pallas kernels, shards(): call(pack_kernel, [bf16(groups, kept_max, LANES), bf16(head // 2, width),...  3.48 us
    pallas_call x1, Pallas kernels, shards(): call(section_kernel, bf16(1, seq_len, width), [VMEM] * 4, HBM, [pltpu.VME...  3.18 us
  transfers between devices with their start and end apart: 5, of which 1 were waited for; matrix products, arithmetic and copies ran while one was open for 0% of the time, Pallas kernels for 42%

profile of v1, /device:TPU:1, one launch (start us, length us, event | category | flops | bytes accessed | tf_op | source)
XLA Modules:
  0.0 59.6 jit_solution(348239908986324791)
XLA Ops:
  0.0 3.5 %shard_map.118 = (bf16[32,32,640]{2,1,0:T(8,128)(2,1)}, bf16[64,6144]{1,0:T(8,128)(2,1)}, f32[8,128]{1,0:T(8,128)}) custom-call(s32[2,16]{1,0:T(2,128)} %bitcast.13, s32[1,16]{1,0:T(1,128)} %count_hbm.1, s32[1,16]{1,0:T(1,128)} %dest_hbm.1, s32[16,32]{1,0:T(8,128)} %bitcast.12, bf16[16,64,588]{2,1,0:T(8,128)(2,1)} %bitcast.11, bf16[128,6144]{1,0:T(8,128)(2,1)} %bitcast.10), custom_call_target="tpu_custom_call" | custom-call | flops 41943040 | bytes 1048576 | tf_op jit(solution)/shard_map/pallas_call | solution.py:313
  3.5 0.0 slice-start
  3.5 0.0 copy-start.5
  3.5 0.0 copy-start.6
  3.5 9.7 %all-to-all-start = ((bf16[32,32,640]{2,1,0:T(8,128)(2,1)}), bf16[32,32,640]{2,1,0:T(8,128)(2,1)S(1)}, u32[]{:S(2)}, u32[]{:S(2)}) async-start(bf16[32,32,640]{2,1,0:T(8,128)(2,1)} %get-tuple-element.14), calls=%async_computation | async-start | bytes 2621440 | tf_op jit(solution)/shard_map/all_to_all | solution.py:330
  13.3 1.3 %collective-permute-start.1 = (bf16[64,6144]{1,0:T(8,128)(2,1)S(1)}, bf16[64,6144]{1,0:T(8,128)(2,1)S(1)}, u32[]{:S(2)}, u32[]{:S(2)}) collective-permute-start(bf16[64,6144]{1,0:T(8,128)(2,1)S(1)} %copy-done.7), channel_id=1, source_target_pairs={{0,1},{1,2},{2,3},{3,0},{4,5},{5,6},{6,7},{7,4},{8,9},{9,10},{10,1... | collective-permute-start | bytes 2359304 | tf_op jit(solution)/shard_map/ppermute | solution.py:332
  14.6 0.1 pad.3.clone
  14.7 0.2 maximum_maximum_fusion.tail_hbm
  14.9 0.0 copy-start
  14.9 3.1 %copy-done = bf16[588,6144]{1,0:T(8,128)(2,1)S(1)} copy-done((bf16[588,6144]{1,0:T(8,128)(2,1)S(1)}, bf16[588,6144]{1,0:T(8,128)(2,1)}, u32[]{:S(2)}) %copy-start) | copy-done | bytes 7225368
  17.9 2.3 %copy-done.1 = bf16[1,6144,384]{2,1,0:T(8,128)(2,1)S(1)} copy-done((bf16[1,6144,384]{2,1,0:T(8,128)(2,1)S(1)}, bf16[1,6144,384]{2,1,0:T(8,128)(2,1)}, u32[]{:S(2)}) %copy-start.1) | copy-done | bytes 4718616
  20.3 6.1 %shard_map.119.weights_hbm = bf16[20480,1024]{1,0:T(8,128)(2,1)} custom-call(f32[8,128]{1,0:T(8,128)S(1)} %copy-done.3, bf16[588,6144]{1,0:T(8,128)(2,1)S(1)} %copy-done, bf16[64,6144]{1,0:T(8,128)(2,1)S(1)} %maximum_maximum_fusion.tail_hbm, bf16[6144,384]{1,0:T(8,128)(2,1)S(1)} %bitcast.8), custom_call_target="tpu_custom_call" | custom-call | flops 1048576 | bytes 1048576 | tf_op jit(solution)/shard_map/pallas_call | solution.py:344
  26.4 0.0 copy-start.2
  26.4 0.0 copy-start.4
  26.4 6.0 %all-to-all-done.recv_ref = bf16[32,32,640]{2,1,0:T(8,128)(2,1)S(1)} async-done(((bf16[32,32,640]{2,1,0:T(8,128)(2,1)}), bf16[32,32,640]{2,1,0:T(8,128)(2,1)S(1)}, u32[]{:S(2)}, u32[]{:S(2)}) %all-to-all-start) | async-done | bytes 1310752 | tf_op jit(solution)/shard_map/all_to_all | solution.py:330
  32.4 1.7 %shard_map.120 = (bf16[512,640]{1,0:T(8,128)(2,1)S(1)}, bf16[2,640,1024]{2,1,0:T(8,128)(2,1)S(1)}) custom-call(bf16[20480,1024]{1,0:T(8,128)(2,1)} %shard_map.119.weights_hbm, bf16[32,32,640]{2,1,0:T(8,128)(2,1)S(1)} %all-to-all-done.recv_ref), custom_call_target="tpu_custom_call" | custom-call | flops 671088640 | bytes 1048576 | tf_op jit(solution)/shard_map/pallas_call | solution.py:353
  34.1 1.5 %collective-permute-start = (bf16[512,640]{1,0:T(8,128)(2,1)S(1)}, bf16[512,640]{1,0:T(8,128)(2,1)S(1)}, u32[]{:S(2)}, u32[]{:S(2)}) collective-permute-start(bf16[512,640]{1,0:T(8,128)(2,1)S(1)} %get-tuple-element.15.x_ref), channel_id=1, source_target_pairs={{0,1},{1,2},{2,3},{3,0},{4,5},{5,6},{6,7},{7,4},{8,9},{9,10},{10,1... | collective-permute-start | bytes 1966088 | tf_op jit(solution)/shard_map/ppermute | solution.py:362
  35.6 0.0 collective-permute-done.1.half_hbm
  35.6 12.0 %shard_map.121 = (bf16[512,128]{1,0:T(8,128)(2,1)S(1)}, bf16[4,640,1024]{2,1,0:T(8,128)(2,1)S(1)}, bf16[64,6144]{1,0:T(8,128)(2,1)S(1)}) custom-call(bf16[512,640]{1,0:T(8,128)(2,1)S(1)} %get-tuple-element.15.x_ref, bf16[1,6144]{1,0:T(2,128)(2,1)S(1)} %copy-done.2, f32[2,128]{1,0:T(2,128)S(1)} %bitcast.9, ...), custom_call_target="tpu_custom_call", output_to_operand_aliasing={{2}: (5, {})} | custom-call | flops 6442450944 | bytes 1048576 | tf_op jit(solution)/shard_map/pallas_call | solution.py:363
  47.6 2.3 %collective-permute-start.3 = (bf16[64,6144]{1,0:T(8,128)(2,1)S(1)}, bf16[64,6144]{1,0:T(8,128)(2,1)S(1)}, u32[]{:S(2)}, u32[]{:S(2)}) collective-permute-start(bf16[64,6144]{1,0:T(8,128)(2,1)S(1)} %get-tuple-element.20.mine_ref), channel_id=1, source_target_pairs={{0,4},{4,0},{8,12},{12,8},{16,20},{20,16},{24,28},{28,24},{32,36},... | collective-permute-start | bytes 2359304 | tf_op jit(solution)/shard_map/ppermute | solution.py:379
  49.9 1.2 %collective-permute-start.2 = (bf16[512,128]{1,0:T(8,128)(2,1)S(1)}, bf16[512,128]{1,0:T(8,128)(2,1)S(1)}, u32[]{:S(2)}, u32[]{:S(2)}) collective-permute-start(bf16[512,128]{1,0:T(8,128)(2,1)S(1)} %get-tuple-element.19), channel_id=1, source_target_pairs={{0,1},{1,2},{2,3},{3,0},{4,5},{5,6},{6,7},{7,4},{8,9},{9,10},{10,1... | collective-permute-start | bytes 393224 | tf_op jit(solution)/shard_map/ppermute | solution.py:378
  51.1 5.1 %shard_map.122.tokens_ref = bf16[512,6144]{1,0:T(8,128)(2,1)S(1)} custom-call(bf16[512,640]{1,0:T(8,128)(2,1)S(1)} %collective-permute-done.x_ref, bf16[2,640,1024]{2,1,0:T(8,128)(2,1)S(1)} %get-tuple-element.16.early_ref, bf16[4,640,1024]{2,1,0:T(8,128)(2,1)S(1)} %get-tuple-element.18.late_ref), custom_call_target="tpu_custom_call" | custom-call | flops 4026531840 | bytes 1048576 | tf_op jit(solution)/shard_map/pallas_call | solution.py:381
  56.2 0.0 collective-permute-done.3.other_ref
  56.2 3.2 %shard_map.123 = bf16[1,512,6144]{2,1,0:T(8,128)(2,1)} custom-call(bf16[512,6144]{1,0:T(8,128)(2,1)S(1)} %shard_map.122.tokens_ref, bf16[512,128]{1,0:T(8,128)(2,1)S(1)} %collective-permute-done.2.attended_ref, bf16[64,6144]{1,0:T(8,128)(2,1)S(1)} %get-tuple-element.20.mine_ref, bf16[64,6144]{1,0:T(8,128)(2,1)S(1)} %collective-permute-done.3.other_ref), custom_call_target="tpu_custom_call" | custom-call | flops 805306368 | bytes 1048576 | tf_op jit(solution)/shard_map/pallas_call | solution.py:390
  (13 shorter events, 0.0 us)
Async XLA Ops:
  3.5 9.8 %copy-start.7 = (bf16[64,6144]{1,0:T(8,128)(2,1)S(1)}, bf16[64,6144]{1,0:T(8,128)(2,1)}, u32[]{:S(2)}) copy-start(bf16[64,6144]{1,0:T(8,128)(2,1)} %get-tuple-element.17) | copy-start | bytes 2359300
  3.5 11.2 %slice-start = ((bf16[588,6144]{1,0:T(8,128)(2,1)}), bf16[12,6144]{1,0:T(8,128)(2,1)S(1)}, s32[]{:S(2)}) async-start(bf16[588,6144]{1,0:T(8,128)(2,1)} %embed_hbm.1), calls=%async_computation.1 | async-start | bytes 393216 | tf_op jit(solution)/shard_map/slice | solution.py:335
  3.5 11.2 %copy-start.5 = (bf16[8,6144]{1,0:T(8,128)(2,1)S(1)}, bf16[8,6144]{1,0:T(8,128)(2,1)}, u32[]{:S(2)}) copy-start(bf16[8,6144]{1,0:T(8,128)(2,1)} %param.19) | copy-start | bytes 294916
  3.5 11.2 %copy-start.6 = (bf16[8,6144]{1,0:T(8,128)(2,1)S(1)}, bf16[8,6144]{1,0:T(8,128)(2,1)}, u32[]{:S(2)}) copy-start(bf16[8,6144]{1,0:T(8,128)(2,1)} %param.18) | copy-start | bytes 294916
  3.5 11.3 %copy-start.3 = (f32[8,128]{1,0:T(8,128)S(1)}, f32[8,128]{1,0:T(8,128)}, u32[]{:S(2)}) copy-start(f32[8,128]{1,0:T(8,128)} %get-tuple-element.13.token_hbm) | copy-start | bytes 12292
  3.5 28.8 %all-to-all-start = ((bf16[32,32,640]{2,1,0:T(8,128)(2,1)}), bf16[32,32,640]{2,1,0:T(8,128)(2,1)S(1)}, u32[]{:S(2)}, u32[]{:S(2)}) async-start(bf16[32,32,640]{2,1,0:T(8,128)(2,1)} %get-tuple-element.14), calls=%async_computation | async-start | bytes 2621440 | tf_op jit(solution)/shard_map/all_to_all | solution.py:330
  13.3 22.3 %collective-permute-start.1 = (bf16[64,6144]{1,0:T(8,128)(2,1)S(1)}, bf16[64,6144]{1,0:T(8,128)(2,1)S(1)}, u32[]{:S(2)}, u32[]{:S(2)}) collective-permute-start(bf16[64,6144]{1,0:T(8,128)(2,1)S(1)} %copy-done.7), channel_id=1, source_target_pairs={{0,1},{1,2},{2,3},{3,0},{4,5},{5,6},{6,7},{7,4},{8,9},{9,10},{10,1... | collective-permute-start | bytes 2359304 | tf_op jit(solution)/shard_map/ppermute | solution.py:332
  14.9 3.1 %copy-start = (bf16[588,6144]{1,0:T(8,128)(2,1)S(1)}, bf16[588,6144]{1,0:T(8,128)(2,1)}, u32[]{:S(2)}) copy-start(bf16[588,6144]{1,0:T(8,128)(2,1)} %embed_hbm.1) | copy-start | bytes 21676036
  17.9 2.3 %copy-start.1 = (bf16[1,6144,384]{2,1,0:T(8,128)(2,1)S(1)}, bf16[1,6144,384]{2,1,0:T(8,128)(2,1)}, u32[]{:S(2)}) copy-start(bf16[1,6144,384]{2,1,0:T(8,128)(2,1)} %param.21) | copy-start | bytes 14155780
  26.4 9.2 %copy-start.2 = (bf16[1,6144]{1,0:T(2,128)(2,1)S(1)}, bf16[1,6144]{1,0:T(2,128)(2,1)}, u32[]{:S(2)}) copy-start(bf16[1,6144]{1,0:T(2,128)(2,1)} %gain_ref.1) | copy-start | bytes 36868
  26.4 9.2 %copy-start.4 = (f32[1,2,128]{2,1,0:T(2,128)S(1)}, f32[1,2,128]{2,1,0:T(2,128)}, u32[]{:S(2)}) copy-start(f32[1,2,128]{2,1,0:T(2,128)} %param.22) | copy-start | bytes 3076
  34.1 17.0 %collective-permute-start = (bf16[512,640]{1,0:T(8,128)(2,1)S(1)}, bf16[512,640]{1,0:T(8,128)(2,1)S(1)}, u32[]{:S(2)}, u32[]{:S(2)}) collective-permute-start(bf16[512,640]{1,0:T(8,128)(2,1)S(1)} %get-tuple-element.15.x_ref), channel_id=1, source_target_pairs={{0,1},{1,2},{2,3},{3,0},{4,5},{5,6},{6,7},{7,4},{8,9},{9,10},{10,1... | collective-permute-start | bytes 1966088 | tf_op jit(solution)/shard_map/ppermute | solution.py:362
  47.6 8.6 %collective-permute-start.3 = (bf16[64,6144]{1,0:T(8,128)(2,1)S(1)}, bf16[64,6144]{1,0:T(8,128)(2,1)S(1)}, u32[]{:S(2)}, u32[]{:S(2)}) collective-permute-start(bf16[64,6144]{1,0:T(8,128)(2,1)S(1)} %get-tuple-element.20.mine_ref), channel_id=1, source_target_pairs={{0,4},{4,0},{8,12},{12,8},{16,20},{20,16},{24,28},{28,24},{32,36},... | collective-permute-start | bytes 2359304 | tf_op jit(solution)/shard_map/ppermute | solution.py:379
  49.9 6.3 %collective-permute-start.2 = (bf16[512,128]{1,0:T(8,128)(2,1)S(1)}, bf16[512,128]{1,0:T(8,128)(2,1)S(1)}, u32[]{:S(2)}, u32[]{:S(2)}) collective-permute-start(bf16[512,128]{1,0:T(8,128)(2,1)S(1)} %get-tuple-element.19), channel_id=1, source_target_pairs={{0,1},{1,2},{2,3},{3,0},{4,5},{5,6},{6,7},{7,4},{8,9},{9,10},{10,1... | collective-permute-start | bytes 393224 | tf_op jit(solution)/shard_map/ppermute | solution.py:378

commit v2 on v1

--- a/solution.py
+++ b/solution.py
@@ -14,8 +14,9 @@
 COL_AT = 596 - TAIL
 SRC_AT = 604 - TAIL
 SRC_END = 636 - TAIL
+SIDE_MIN = 6
+SIDE_MAX = 8
 TILE = 1024
-EARLY = 2
 STORE = 20480
 MIB = 1 << 20
 
@@ -65,17 +66,22 @@
     number = iota((patch_max, 128), 0)
     lane = iota((patch_max, 128), 1)
     source = lane == SRC_AT + device
+    flags = {}
+    for width in range(SIDE_MIN, SIDE_MAX + 1):
+        row = jnp.zeros_like(number)
+        for k in range(1, SIDE_MAX):
+            row = row + (number >= k * width).astype(jnp.int32)
+        col = number - row * width
+        flags[width] = ((lane == ROW_AT + row) | (lane == COL_AT + col) | source).astype(jnp.float32)
     for copy in small:
         copy.wait()
     for g in range(images):
         if g % step == 0:
             large[g // step].wait()
         width = shape[1, g]
-        row = jnp.zeros_like(number)
-        for k in range(1, 8):
-            row = row + (number >= k * width).astype(jnp.int32)
-        col = number - row * width
-        flags = as_bf16((lane == ROW_AT + row) | (lane == COL_AT + col) | source)
+        own = flags[SIDE_MAX]
+        for side in range(SIDE_MIN, SIDE_MAX):
+            own = jnp.where(width == side, flags[side], own)
         picked = (iota((patch_max, kept_max), 0) == keep[g : g + 1, :]) & (
             iota((patch_max, kept_max), 1) < count[0, g]
         )
@@ -83,15 +89,12 @@
         there = dest[0, g]
         body = dot(picked, patches[g, :, :TAIL], ((0,), (0,)))
         out_ref[there, :, :TAIL] = body.astype(jnp.bfloat16)
-        last = jnp.concatenate([patches[g, :, TAIL:], flags[:, ROW_AT:]], axis=1)
+        last = jnp.concatenate([patches[g, :, TAIL:], own.astype(jnp.bfloat16)[:, ROW_AT:]], axis=1)
         out_ref[there, :, TAIL:] = dot(picked, last, ((0,), (0,))).astype(jnp.bfloat16)
     half.wait()
 
 
-def compact_kernel(weights_hbm, recv_ref, out_ref, early_ref, sems):
-    copies = tile_copies(weights_hbm, 0, early_ref, sems)
-    for copy in copies:
-        copy.start()
+def compact_kernel(weights_hbm, recv_ref, out_ref):
     sources, kept_max, lanes = recv_ref.shape
     total = sources * kept_max
     blocks = total // 128
@@ -114,8 +117,6 @@
     slot = iota((seq_len, 128), 0)
     hot = jnp.concatenate([as_bf16(slot == place[b : b + 1, :]) for b in range(blocks)], axis=1)
     out_ref[...] = dot(hot, received).astype(jnp.bfloat16)
-    for copy in copies:
-        copy.wait()
 
 
 def lane_sums(values, sums):
@@ -168,42 +169,40 @@
     return weights.at[pl.ds(first, qkv.shape[0]), pl.ds(0, qkv.shape[1])]
 
 
-def tile_copies(weights_hbm, first, embed, sems):
+def tile_copies(weights_hbm, embed, sems):
     tiles, lanes, _ = embed.shape
     return [
-        pltpu.make_async_copy(weights_hbm.at[pl.ds((first + t) * lanes, lanes)], embed.at[t], sems.at[t])
+        pltpu.make_async_copy(weights_hbm.at[pl.ds(t * lanes, lanes)], embed.at[t], sems.at[t])
         for t in range(tiles)
     ]
 
 
 def attend_kernel(
-    x_ref, gain_ref, norm_ref, early_ref, weights_hbm, half_hbm,
-    out_ref, late_ref, same_half_hbm, tokens, qkv, sems, qkv_sem,
+    x_ref, gain_ref, norm_ref, weights_hbm, half_hbm,
+    out_ref, embed, same_half_hbm, tokens, qkv, sems, qkv_sem,
 ):
-    early, late = early_ref.shape[0], late_ref.shape[0]
-    copies = tile_copies(weights_hbm, early, late_ref, sems)
-    for copy in copies:
-        copy.start()
-    lanes = late_ref.shape[1]
-    qkv_copy = pltpu.make_async_copy(
-        qkv_part(weights_hbm, (early + late) * lanes, qkv), qkv, qkv_sem.at[0]
-    )
-    width = (early + late) * TILE
+    tiles, lanes, _ = embed.shape
+    copies = tile_copies(weights_hbm, embed, sems)
+    qkv_copy = pltpu.make_async_copy(qkv_part(weights_hbm, tiles * lanes, qkv), qkv, qkv_sem.at[0])
+    width = tiles * TILE
+    copies[0].start()
+    copies[1].start()
     x = x_ref[...]
     rows = x.shape[0]
     spans = [slice(at, at + TILE) for at in range(0, width, TILE)]
     total = jnp.zeros((rows, 128), jnp.float32)
     squares = jnp.zeros((rows, 128), jnp.float32)
     for t, span in enumerate(spans):
-        if t == early:
-            copies[0].wait()
-            copies[1].wait()
-            qkv_copy.start()
-        if t == early + 2:
-            for copy in copies[2:]:
-                copy.wait()
-        tile = early_ref[t] if t < early else late_ref[t - early]
-        part = dot(x, tile).astype(jnp.bfloat16)
+        if t < 2:
+            copies[t].wait()
+            for later in copies[2 * t + 2 : 2 * t + 4]:
+                later.start()
+        elif t % 2 == 0:
+            copies[t].wait()
+            copies[t + 1].wait()
+            if t == 2:
+                qkv_copy.start()
+        part = dot(x, embed[t]).astype(jnp.bfloat16)
         tokens[:, span] = part
         part = part.astype(jnp.float32)
         total = lane_sums(part, total)
@@ -226,19 +225,23 @@
     flags = jnp.where((lane >= SRC_AT) & (lane < SRC_END), flags, 0.0)
     live = jnp.sum(flags, axis=1, keepdims=True) > 0.5
     flags = flags.astype(jnp.bfloat16)
-    same = dot(flags, flags, ((1,), (1,))) > 0.5
-    scores = dot(queries, keys, ((1,), (1,))) / math.sqrt(head)
-    scores = jnp.where(same, scores, -1e30)
-    expo = jnp.exp(scores - jnp.max(scores, axis=1, keepdims=True))
-    weights = (expo / jnp.sum(expo, axis=1, keepdims=True)).astype(jnp.bfloat16)
-    out_ref[...] = jnp.where(live, dot(weights, values), 0.0).astype(jnp.bfloat16)
-
-
-def embed_kernel(x_ref, early_ref, late_ref, out_ref):
-    early, late = early_ref.shape[0], late_ref.shape[0]
-    for t in range(early + late):
-        tile = early_ref[t] if t < early else late_ref[t - early]
-        out_ref[:, t * TILE : (t + 1) * TILE] = dot(x_ref[...], tile).astype(jnp.bfloat16)
+    for at in range(0, rows, 128):
+        here = slice(at, at + 128)
+        first = min(max(at - 64, 0), rows - 256)
+        near = slice(first, first + 256)
+        same = dot(flags[here], flags[near], ((1,), (1,))) > 0.5
+        scores = dot(queries[here], keys[near], ((1,), (1,))) * (1.0 / math.sqrt(head))
+        scores = jnp.where(same, scores, -1e30)
+        expo = jnp.exp(scores - jnp.max(scores, axis=1, keepdims=True))
+        weights = (expo * (1.0 / jnp.sum(expo, axis=1, keepdims=True))).astype(jnp.bfloat16)
+        attended = jnp.where(live[here], dot(weights, values[near]), 0.0)
+        out_ref[here, :] = attended.astype(jnp.bfloat16)
+
+
+def embed_kernel(x_ref, embed_ref, out_ref):
+    for t in range(embed_ref.shape[0]):
+        span = slice(t * TILE, (t + 1) * TILE)
+        out_ref[:, span] = dot(x_ref[...], embed_ref[t]).astype(jnp.bfloat16)
 
 
 def section_kernel(
@@ -350,43 +353,43 @@
         20,
         MIB,
     )(after_pack, embed_weight, tail, qkv_weight[0])
-    x, first_tiles = call(
+    x = call(
         compact_kernel,
-        [bf16(seq_len, LANES), bf16(EARLY, LANES, TILE)],
+        bf16(seq_len, LANES),
         [HBM, VMEM],
-        [VMEM] * 2,
-        [dma((EARLY,))],
+        VMEM,
+        [],
         16,
         2 * seq_len * groups * kept_max * LANES,
     )(weights, received)
     next_x = lax.ppermute(x, "segment", onward)
-    attended, other_tiles, half = call(
+    attended, embed, half = call(
         attend_kernel,
-        [bf16(seq_len, head), bf16(tiles - EARLY, LANES, TILE), bf16(head // 2, width)],
-        [VMEM] * 4 + [HBM] * 2,
+        [bf16(seq_len, head), bf16(tiles, LANES, TILE), bf16(head // 2, width)],
+        [VMEM] * 3 + [HBM] * 2,
         [VMEM, VMEM, HBM],
         [
             pltpu.VMEM((seq_len, width), jnp.bfloat16),
             qkv_scratch,
-            dma((tiles - EARLY,)),
+            dma((tiles,)),
             dma((1,)),
         ],
         34,
         2 * seq_len * width * (LANES + 3 * head),
-        {5: 2},
-    )(x, ln_gain, norm_gains[0], first_tiles, weights, half)
+        {4: 2},
+    )(x, ln_gain, norm_gains[0], weights, half)
     next_attended = lax.ppermute(attended, "segment", onward)
     other = lax.ppermute(half, "dp", pairs)
 
     tokens = call(
         embed_kernel,
         bf16(seq_len, width),
-        [VMEM] * 3,
+        [VMEM] * 2,
         VMEM,
         [],
         16,
         2 * seq_len * width * LANES,
-    )(next_x, first_tiles, other_tiles)
+    )(next_x, embed)
     return call(
         section_kernel,
         bf16(1, seq_len, width),

time: 60.1 us -> 59.8 us (level)
  no operation moved by 1% of the time
where the time goes in v2:
time: 59.8 us; the launch traced here: 59.5 us
  Pallas kernels  31.5 us (53%)
  starting transfers between devices  16 us (27%)
  waiting for transfers between devices  5.98 us (10%)
  local copies, waits for them, and re-layouts  5.52 us (9%)
    pallas_call x1, Pallas kernels, shards(): call(attend_kernel, [bf16(seq_len, head), bf16(tiles, LANES, TILE), bf16(...  12.5 us
    all_to_all x1, starting transfers between devices, shards(): lax.all_to_all(packed, 'dp', split_axis=0, concat_axis=0, tiled=True)  9.74 us
    pallas_call x1, Pallas kernels, shards(): call(weight_kernel, bf16(STORE, TILE), [HBM] * 4, HBM, [embed_scratch, qk...  6.12 us
    all_to_all x1, waiting for transfers between devices, shards(): lax.all_to_all(packed, 'dp', split_axis=0, concat_axis=0, tiled=True)  5.97 us
    unnamed x16, local copies, waits for them, and re-layouts  5.43 us
    pallas_call x1, Pallas kernels, shards(): call(embed_kernel, bf16(seq_len, width), [VMEM] * 2, VMEM, [], 16, 2 * se...  5.11 us
    pallas_call x1, Pallas kernels, shards(): call(pack_kernel, [bf16(groups, kept_max, LANES), bf16(head // 2, width),...  3.34 us
    pallas_call x1, Pallas kernels, shards(): call(section_kernel, bf16(1, seq_len, width), [VMEM] * 4, HBM, [pltpu.VME...  3.18 us
  transfers between devices with their start and end apart: 5, of which 1 were waited for; matrix products, arithmetic and copies ran while one was open for 0% of the time, Pallas kernels for 42%

profile of v2, /device:TPU:1, one launch (start us, length us, event | category | flops | bytes accessed | tf_op | source)
XLA Modules:
  0.0 59.5 jit_solution(7352669686887298388)
XLA Ops:
  0.0 3.3 %shard_map.118 = (bf16[32,32,640]{2,1,0:T(8,128)(2,1)}, bf16[64,6144]{1,0:T(8,128)(2,1)}, f32[8,128]{1,0:T(8,128)}) custom-call(s32[2,16]{1,0:T(2,128)} %bitcast.13, s32[1,16]{1,0:T(1,128)} %count_hbm.1, s32[1,16]{1,0:T(1,128)} %dest_hbm.1, s32[16,32]{1,0:T(8,128)} %bitcast.12, bf16[16,64,588]{2,1,0:T(8,128)(2,1)} %bitcast.11, bf16[128,6144]{1,0:T(8,128)(2,1)} %bitcast.10), custom_call_target="tpu_custom_call" | custom-call | flops 41943040 | bytes 1048576 | tf_op jit(solution)/shard_map/pallas_call | solution.py:316
  3.4 0.0 slice-start
  3.4 0.0 copy-start.5
  3.4 0.0 copy-start.6
  3.4 9.7 %all-to-all-start = ((bf16[32,32,640]{2,1,0:T(8,128)(2,1)}), bf16[32,32,640]{2,1,0:T(8,128)(2,1)S(1)}, u32[]{:S(2)}, u32[]{:S(2)}) async-start(bf16[32,32,640]{2,1,0:T(8,128)(2,1)} %get-tuple-element.12), calls=%async_computation | async-start | bytes 2621440 | tf_op jit(solution)/shard_map/all_to_all | solution.py:333
  13.2 1.3 %collective-permute-start.1 = (bf16[64,6144]{1,0:T(8,128)(2,1)S(1)}, bf16[64,6144]{1,0:T(8,128)(2,1)S(1)}, u32[]{:S(2)}, u32[]{:S(2)}) collective-permute-start(bf16[64,6144]{1,0:T(8,128)(2,1)S(1)} %copy-done.7), channel_id=1, source_target_pairs={{0,1},{1,2},{2,3},{3,0},{4,5},{5,6},{6,7},{7,4},{8,9},{9,10},{10,1... | collective-permute-start | bytes 2359304 | tf_op jit(solution)/shard_map/ppermute | solution.py:335
  14.5 0.1 pad.3.clone
  14.5 0.2 maximum_maximum_fusion.tail_hbm
  14.7 0.0 copy-start
  14.7 3.1 %copy-done = bf16[588,6144]{1,0:T(8,128)(2,1)S(1)} copy-done((bf16[588,6144]{1,0:T(8,128)(2,1)S(1)}, bf16[588,6144]{1,0:T(8,128)(2,1)}, u32[]{:S(2)}) %copy-start) | copy-done | bytes 7225368
  17.8 2.3 %copy-done.1 = bf16[1,6144,384]{2,1,0:T(8,128)(2,1)S(1)} copy-done((bf16[1,6144,384]{2,1,0:T(8,128)(2,1)S(1)}, bf16[1,6144,384]{2,1,0:T(8,128)(2,1)}, u32[]{:S(2)}) %copy-start.1) | copy-done | bytes 4718616
  20.1 6.1 %shard_map.119.weights_hbm = bf16[20480,1024]{1,0:T(8,128)(2,1)} custom-call(f32[8,128]{1,0:T(8,128)S(1)} %copy-done.3, bf16[588,6144]{1,0:T(8,128)(2,1)S(1)} %copy-done, bf16[64,6144]{1,0:T(8,128)(2,1)S(1)} %maximum_maximum_fusion.tail_hbm, bf16[6144,384]{1,0:T(8,128)(2,1)S(1)} %bitcast.8), custom_call_target="tpu_custom_call" | custom-call | flops 1048576 | bytes 1048576 | tf_op jit(solution)/shard_map/pallas_call | solution.py:347
  26.2 0.0 copy-start.2
  26.3 0.0 copy-start.4
  26.3 6.0 %all-to-all-done.recv_ref = bf16[32,32,640]{2,1,0:T(8,128)(2,1)S(1)} async-done(((bf16[32,32,640]{2,1,0:T(8,128)(2,1)}), bf16[32,32,640]{2,1,0:T(8,128)(2,1)S(1)}, u32[]{:S(2)}, u32[]{:S(2)}) %all-to-all-start) | async-done | bytes 1310752 | tf_op jit(solution)/shard_map/all_to_all | solution.py:333
  32.2 1.3 %shard_map.120.x_ref = bf16[512,640]{1,0:T(8,128)(2,1)S(1)} custom-call(bf16[20480,1024]{1,0:T(8,128)(2,1)} %shard_map.119.weights_hbm, bf16[32,32,640]{2,1,0:T(8,128)(2,1)S(1)} %all-to-all-done.recv_ref), custom_call_target="tpu_custom_call" | custom-call | flops 671088640 | bytes 1048576 | tf_op jit(solution)/shard_map/pallas_call | solution.py:356
  33.5 1.5 %collective-permute-start = (bf16[512,640]{1,0:T(8,128)(2,1)S(1)}, bf16[512,640]{1,0:T(8,128)(2,1)S(1)}, u32[]{:S(2)}, u32[]{:S(2)}) collective-permute-start(bf16[512,640]{1,0:T(8,128)(2,1)S(1)} %shard_map.120.x_ref), channel_id=1, source_target_pairs={{0,1},{1,2},{2,3},{3,0},{4,5},{5,6},{6,7},{7,4},{8,9},{9,10},{10,1... | collective-permute-start | bytes 1966088 | tf_op jit(solution)/shard_map/ppermute | solution.py:365
  35.0 0.0 collective-permute-done.1.half_hbm
  35.0 12.5 %shard_map.121 = (bf16[512,128]{1,0:T(8,128)(2,1)S(1)}, bf16[6,640,1024]{2,1,0:T(8,128)(2,1)S(1)}, bf16[64,6144]{1,0:T(8,128)(2,1)S(1)}) custom-call(bf16[512,640]{1,0:T(8,128)(2,1)S(1)} %shard_map.120.x_ref, bf16[1,6144]{1,0:T(2,128)(2,1)S(1)} %copy-done.2, f32[2,128]{1,0:T(2,128)S(1)} %bitcast.9, ...), custom_call_target="tpu_custom_call", output_to_operand_aliasing={{2}: (4, {})} | custom-call | flops 6442450944 | bytes 1048576 | tf_op jit(solution)/shard_map/pallas_call | solution.py:366
  47.4 2.3 %collective-permute-start.3 = (bf16[64,6144]{1,0:T(8,128)(2,1)S(1)}, bf16[64,6144]{1,0:T(8,128)(2,1)S(1)}, u32[]{:S(2)}, u32[]{:S(2)}) collective-permute-start(bf16[64,6144]{1,0:T(8,128)(2,1)S(1)} %get-tuple-element.16.mine_ref), channel_id=1, source_target_pairs={{0,4},{4,0},{8,12},{12,8},{16,20},{20,16},{24,28},{28,24},{32,36},... | collective-permute-start | bytes 2359304 | tf_op jit(solution)/shard_map/ppermute | solution.py:382
  49.7 1.2 %collective-permute-start.2 = (bf16[512,128]{1,0:T(8,128)(2,1)S(1)}, bf16[512,128]{1,0:T(8,128)(2,1)S(1)}, u32[]{:S(2)}, u32[]{:S(2)}) collective-permute-start(bf16[512,128]{1,0:T(8,128)(2,1)S(1)} %get-tuple-element.15), channel_id=1, source_target_pairs={{0,1},{1,2},{2,3},{3,0},{4,5},{5,6},{6,7},{7,4},{8,9},{9,10},{10,1... | collective-permute-start | bytes 393224 | tf_op jit(solution)/shard_map/ppermute | solution.py:381
  51.0 0.0 collective-permute-done.x_ref
  51.0 5.1 %shard_map.122.tokens_ref = bf16[512,6144]{1,0:T(8,128)(2,1)S(1)} custom-call(bf16[512,640]{1,0:T(8,128)(2,1)S(1)} %collective-permute-done.x_ref, bf16[6,640,1024]{2,1,0:T(8,128)(2,1)S(1)} %get-tuple-element.14.embed_ref), custom_call_target="tpu_custom_call" | custom-call | flops 4026531840 | bytes 1048576 | tf_op jit(solution)/shard_map/pallas_call | solution.py:384
  56.1 3.2 %shard_map.123 = bf16[1,512,6144]{2,1,0:T(8,128)(2,1)} custom-call(bf16[512,6144]{1,0:T(8,128)(2,1)S(1)} %shard_map.122.tokens_ref, bf16[512,128]{1,0:T(8,128)(2,1)S(1)} %collective-permute-done.2.attended_ref, bf16[64,6144]{1,0:T(8,128)(2,1)S(1)} %get-tuple-element.16.mine_ref, bf16[64,6144]{1,0:T(8,128)(2,1)S(1)} %collective-permute-done.3.other_ref), custom_call_target="tpu_custom_call" | custom-call | flops 805306368 | bytes 1048576 | tf_op jit(solution)/shard_map/pallas_call | solution.py:393
  (13 shorter events, 0.0 us)
Async XLA Ops:
  3.3 9.8 %copy-start.7 = (bf16[64,6144]{1,0:T(8,128)(2,1)S(1)}, bf16[64,6144]{1,0:T(8,128)(2,1)}, u32[]{:S(2)}) copy-start(bf16[64,6144]{1,0:T(8,128)(2,1)} %get-tuple-element.13) | copy-start | bytes 2359300
  3.4 11.2 %slice-start = ((bf16[588,6144]{1,0:T(8,128)(2,1)}), bf16[12,6144]{1,0:T(8,128)(2,1)S(1)}, s32[]{:S(2)}) async-start(bf16[588,6144]{1,0:T(8,128)(2,1)} %embed_hbm.1), calls=%async_computation.1 | async-start | bytes 393216 | tf_op jit(solution)/shard_map/slice | solution.py:338
  3.4 11.2 %copy-start.5 = (bf16[8,6144]{1,0:T(8,128)(2,1)S(1)}, bf16[8,6144]{1,0:T(8,128)(2,1)}, u32[]{:S(2)}) copy-start(bf16[8,6144]{1,0:T(8,128)(2,1)} %param.19) | copy-start | bytes 294916
  3.4 11.2 %copy-start.6 = (bf16[8,6144]{1,0:T(8,128)(2,1)S(1)}, bf16[8,6144]{1,0:T(8,128)(2,1)}, u32[]{:S(2)}) copy-start(bf16[8,6144]{1,0:T(8,128)(2,1)} %param.18) | copy-start | bytes 294916
  3.4 11.3 %copy-start.3 = (f32[8,128]{1,0:T(8,128)S(1)}, f32[8,128]{1,0:T(8,128)}, u32[]{:S(2)}) copy-start(f32[8,128]{1,0:T(8,128)} %get-tuple-element.11.token_hbm) | copy-start | bytes 12292
  3.4 28.8 %all-to-all-start = ((bf16[32,32,640]{2,1,0:T(8,128)(2,1)}), bf16[32,32,640]{2,1,0:T(8,128)(2,1)S(1)}, u32[]{:S(2)}, u32[]{:S(2)}) async-start(bf16[32,32,640]{2,1,0:T(8,128)(2,1)} %get-tuple-element.12), calls=%async_computation | async-start | bytes 2621440 | tf_op jit(solution)/shard_map/all_to_all | solution.py:333
  13.2 21.8 %collective-permute-start.1 = (bf16[64,6144]{1,0:T(8,128)(2,1)S(1)}, bf16[64,6144]{1,0:T(8,128)(2,1)S(1)}, u32[]{:S(2)}, u32[]{:S(2)}) collective-permute-start(bf16[64,6144]{1,0:T(8,128)(2,1)S(1)} %copy-done.7), channel_id=1, source_target_pairs={{0,1},{1,2},{2,3},{3,0},{4,5},{5,6},{6,7},{7,4},{8,9},{9,10},{10,1... | collective-permute-start | bytes 2359304 | tf_op jit(solution)/shard_map/ppermute | solution.py:335
  14.7 3.1 %copy-start = (bf16[588,6144]{1,0:T(8,128)(2,1)S(1)}, bf16[588,6144]{1,0:T(8,128)(2,1)}, u32[]{:S(2)}) copy-start(bf16[588,6144]{1,0:T(8,128)(2,1)} %embed_hbm.1) | copy-start | bytes 21676036
  17.8 2.3 %copy-start.1 = (bf16[1,6144,384]{2,1,0:T(8,128)(2,1)S(1)}, bf16[1,6144,384]{2,1,0:T(8,128)(2,1)}, u32[]{:S(2)}) copy-start(bf16[1,6144,384]{2,1,0:T(8,128)(2,1)} %param.21) | copy-start | bytes 14155780
  26.2 8.7 %copy-start.2 = (bf16[1,6144]{1,0:T(2,128)(2,1)S(1)}, bf16[1,6144]{1,0:T(2,128)(2,1)}, u32[]{:S(2)}) copy-start(bf16[1,6144]{1,0:T(2,128)(2,1)} %gain_ref.1) | copy-start | bytes 36868
  26.3 8.7 %copy-start.4 = (f32[1,2,128]{2,1,0:T(2,128)S(1)}, f32[1,2,128]{2,1,0:T(2,128)}, u32[]{:S(2)}) copy-start(f32[1,2,128]{2,1,0:T(2,128)} %param.22) | copy-start | bytes 3076
  33.5 17.5 %collective-permute-start = (bf16[512,640]{1,0:T(8,128)(2,1)S(1)}, bf16[512,640]{1,0:T(8,128)(2,1)S(1)}, u32[]{:S(2)}, u32[]{:S(2)}) collective-permute-start(bf16[512,640]{1,0:T(8,128)(2,1)S(1)} %shard_map.120.x_ref), channel_id=1, source_target_pairs={{0,1},{1,2},{2,3},{3,0},{4,5},{5,6},{6,7},{7,4},{8,9},{9,10},{10,1... | collective-permute-start | bytes 1966088 | tf_op jit(solution)/shard_map/ppermute | solution.py:365
  47.4 8.7 %collective-permute-start.3 = (bf16[64,6144]{1,0:T(8,128)(2,1)S(1)}, bf16[64,6144]{1,0:T(8,128)(2,1)S(1)}, u32[]{:S(2)}, u32[]{:S(2)}) collective-permute-start(bf16[64,6144]{1,0:T(8,128)(2,1)S(1)} %get-tuple-element.16.mine_ref), channel_id=1, source_target_pairs={{0,4},{4,0},{8,12},{12,8},{16,20},{20,16},{24,28},{28,24},{32,36},... | collective-permute-start | bytes 2359304 | tf_op jit(solution)/shard_map/ppermute | solution.py:382
  49.7 6.3 %collective-permute-start.2 = (bf16[512,128]{1,0:T(8,128)(2,1)S(1)}, bf16[512,128]{1,0:T(8,128)(2,1)S(1)}, u32[]{:S(2)}, u32[]{:S(2)}) collective-permute-start(bf16[512,128]{1,0:T(8,128)(2,1)S(1)} %get-tuple-element.15), channel_id=1, source_target_pairs={{0,1},{1,2},{2,3},{3,0},{4,5},{5,6},{6,7},{7,4},{8,9},{9,10},{10,1... | collective-permute-start | bytes 393224 | tf_op jit(solution)/shard_map/ppermute | solution.py:381

commit v3 on v2

--- a/solution.py
+++ b/solution.py
@@ -241,21 +241,23 @@
 def embed_kernel(x_ref, embed_ref, out_ref):
     for t in range(embed_ref.shape[0]):
         span = slice(t * TILE, (t + 1) * TILE)
-        out_ref[:, span] = dot(x_ref[...], embed_ref[t]).astype(jnp.bfloat16)
+        out_ref[:, span] = dot(x_ref[:, :TAIL], embed_ref[t, :TAIL])
 
 
 def section_kernel(
-    tokens_ref, attended_ref, mine_ref, other_ref, out_hbm, weight, out, sems
+    part_ref, x_ref, attended_ref, embed_ref, mine_ref, other_ref, out_hbm, weight, out, sems
 ):
     half = mine_ref.shape[0]
+    last = x_ref.shape[1] - TAIL
     core = lax.axis_index("dp") % 2
-    weight[pl.ds(pl.multiple_of(core * half, half), half), :] = mine_ref[...]
-    weight[pl.ds(pl.multiple_of((1 - core) * half, half), half), :] = other_ref[...]
+    weight[pl.ds(pl.multiple_of(last + core * half, half), half), :] = mine_ref[...]
+    weight[pl.ds(pl.multiple_of(last + (1 - core) * half, half), half), :] = other_ref[...]
+    both = jnp.concatenate([x_ref[:, TAIL:], attended_ref[...]], axis=1)
     results = []
     for t in range(out.shape[1] // TILE):
         span = slice(t * TILE, (t + 1) * TILE)
-        part = tokens_ref[:, span].astype(jnp.float32)
-        out[:, span] = (part + dot(attended_ref[...], weight[:, span])).astype(jnp.bfloat16)
+        weight[:last, span] = embed_ref[t, TAIL:]
+        out[:, span] = (part_ref[:, span] + dot(both, weight[:, span])).astype(jnp.bfloat16)
         columns = pl.ds(t * TILE, TILE)
         result = pltpu.make_async_copy(out.at[:, columns], out_hbm.at[0, :, columns], sems.at[t])
         result.start()
@@ -381,28 +383,28 @@
     next_attended = lax.ppermute(attended, "segment", onward)
     other = lax.ppermute(half, "dp", pairs)
 
-    tokens = call(
+    part = call(
         embed_kernel,
-        bf16(seq_len, width),
+        jax.ShapeDtypeStruct((seq_len, width), jnp.float32),
         [VMEM] * 2,
         VMEM,
         [],
-        16,
+        24,
         2 * seq_len * width * LANES,
     )(next_x, embed)
     return call(
         section_kernel,
         bf16(1, seq_len, width),
-        [VMEM] * 4,
+        [VMEM] * 6,
         HBM,
         [
-            pltpu.VMEM((head, width), jnp.bfloat16),
+            pltpu.VMEM((LANES - TAIL + head, width), jnp.bfloat16),
             pltpu.VMEM((seq_len, width), jnp.bfloat16),
             dma((tiles,)),
         ],
         30,
         2 * seq_len * width * head,
-    )(tokens, next_attended, half, other)
+    )(part, next_x, next_attended, embed, half, other)
 
 
 def solution(mesh):

time: 59.8 us -> 59.5 us (level)
  Pallas kernels: 31.5 us -> 29.8 us
  waiting for transfers between devices: 5.98 us -> 7.29 us
    pallas_call x2, Pallas kernels: 8.29 us -> 6.68 us  [the longest x1 3.47 us: shards(): call(embed_kernel, jax.ShapeDtypeStruct((seq_len, width), jnp.float32), [...]
    ppermute x1, waiting for transfers between devices: 0.01 us -> 1.3 us  [shards(): next_attended = lax.ppermute(attended, 'segment', onward)]
  transfers between devices with their start and end apart: 5 -> 5, of which waited for: 1 -> 2; matrix products, arithmetic and copies ran while one was open for 0% -> 0% of each run, Pallas kernels for 42% -> 39%
where the time goes in v3:
time: 59.5 us; the launch traced here: 59.1 us
  Pallas kernels  29.8 us (50%)
  starting transfers between devices  16 us (27%)
  waiting for transfers between devices  7.29 us (12%)
  local copies, waits for them, and re-layouts  5.52 us (9%)
    pallas_call x1, Pallas kernels, shards(): call(attend_kernel, [bf16(seq_len, head), bf16(tiles, LANES, TILE), bf16(...  12.5 us
    all_to_all x1, starting transfers between devices, shards(): lax.all_to_all(packed, 'dp', split_axis=0, concat_axis=0, tiled=True)  9.74 us
    pallas_call x1, Pallas kernels, shards(): call(weight_kernel, bf16(STORE, TILE), [HBM] * 4, HBM, [embed_scratch, qk...  6.12 us
    all_to_all x1, waiting for transfers between devices, shards(): lax.all_to_all(packed, 'dp', split_axis=0, concat_axis=0, tiled=True)  5.97 us
    unnamed x16, local copies, waits for them, and re-layouts  5.43 us
    pallas_call x1, Pallas kernels, shards(): call(embed_kernel, jax.ShapeDtypeStruct((seq_len, width), jnp.float32), [...  3.47 us
    pallas_call x1, Pallas kernels, shards(): call(pack_kernel, [bf16(groups, kept_max, LANES), bf16(head // 2, width),...  3.34 us
    pallas_call x1, Pallas kernels, shards(): call(section_kernel, bf16(1, seq_len, width), [VMEM] * 6, HBM, [pltpu.VME...  3.21 us
  transfers between devices with their start and end apart: 5, of which 2 were waited for; matrix products, arithmetic and copies ran while one was open for 0% of the time, Pallas kernels for 39%

profile of v3, /device:TPU:1, one launch (start us, length us, event | category | flops | bytes accessed | tf_op | source)
XLA Modules:
  0.0 59.1 jit_solution(7325761281327039757)
XLA Ops:
  0.0 3.3 %shard_map.118 = (bf16[32,32,640]{2,1,0:T(8,128)(2,1)}, bf16[64,6144]{1,0:T(8,128)(2,1)}, f32[8,128]{1,0:T(8,128)}) custom-call(s32[2,16]{1,0:T(2,128)} %bitcast.13, s32[1,16]{1,0:T(1,128)} %count_hbm.1, s32[1,16]{1,0:T(1,128)} %dest_hbm.1, s32[16,32]{1,0:T(8,128)} %bitcast.12, bf16[16,64,588]{2,1,0:T(8,128)(2,1)} %bitcast.11, bf16[128,6144]{1,0:T(8,128)(2,1)} %bitcast.10), custom_call_target="tpu_custom_call" | custom-call | flops 41943040 | bytes 1048576 | tf_op jit(solution)/shard_map/pallas_call | solution.py:318
  3.4 0.0 slice-start
  3.4 0.0 copy-start.5
  3.4 0.0 copy-start.6
  3.4 9.7 %all-to-all-start = ((bf16[32,32,640]{2,1,0:T(8,128)(2,1)}), bf16[32,32,640]{2,1,0:T(8,128)(2,1)S(1)}, u32[]{:S(2)}, u32[]{:S(2)}) async-start(bf16[32,32,640]{2,1,0:T(8,128)(2,1)} %get-tuple-element.12), calls=%async_computation | async-start | bytes 2621440 | tf_op jit(solution)/shard_map/all_to_all | solution.py:335
  13.2 1.3 %collective-permute-start.1 = (bf16[64,6144]{1,0:T(8,128)(2,1)S(1)}, bf16[64,6144]{1,0:T(8,128)(2,1)S(1)}, u32[]{:S(2)}, u32[]{:S(2)}) collective-permute-start(bf16[64,6144]{1,0:T(8,128)(2,1)S(1)} %copy-done.7), channel_id=1, source_target_pairs={{0,1},{1,2},{2,3},{3,0},{4,5},{5,6},{6,7},{7,4},{8,9},{9,10},{10,1... | collective-permute-start | bytes 2359304 | tf_op jit(solution)/shard_map/ppermute | solution.py:337
  14.5 0.1 pad.3.clone
  14.5 0.2 maximum_maximum_fusion.tail_hbm
  14.7 0.0 copy-start
  14.7 3.1 %copy-done = bf16[588,6144]{1,0:T(8,128)(2,1)S(1)} copy-done((bf16[588,6144]{1,0:T(8,128)(2,1)S(1)}, bf16[588,6144]{1,0:T(8,128)(2,1)}, u32[]{:S(2)}) %copy-start) | copy-done | bytes 7225368
  17.8 2.3 %copy-done.1 = bf16[1,6144,384]{2,1,0:T(8,128)(2,1)S(1)} copy-done((bf16[1,6144,384]{2,1,0:T(8,128)(2,1)S(1)}, bf16[1,6144,384]{2,1,0:T(8,128)(2,1)}, u32[]{:S(2)}) %copy-start.1) | copy-done | bytes 4718616
  20.1 6.1 %shard_map.119.weights_hbm = bf16[20480,1024]{1,0:T(8,128)(2,1)} custom-call(f32[8,128]{1,0:T(8,128)S(1)} %copy-done.3, bf16[588,6144]{1,0:T(8,128)(2,1)S(1)} %copy-done, bf16[64,6144]{1,0:T(8,128)(2,1)S(1)} %maximum_maximum_fusion.tail_hbm, bf16[6144,384]{1,0:T(8,128)(2,1)S(1)} %bitcast.8), custom_call_target="tpu_custom_call" | custom-call | flops 1048576 | bytes 1048576 | tf_op jit(solution)/shard_map/pallas_call | solution.py:349
  26.2 0.0 copy-start.2
  26.3 0.0 copy-start.4
  26.3 6.0 %all-to-all-done.recv_ref = bf16[32,32,640]{2,1,0:T(8,128)(2,1)S(1)} async-done(((bf16[32,32,640]{2,1,0:T(8,128)(2,1)}), bf16[32,32,640]{2,1,0:T(8,128)(2,1)S(1)}, u32[]{:S(2)}, u32[]{:S(2)}) %all-to-all-start) | async-done | bytes 1310752 | tf_op jit(solution)/shard_map/all_to_all | solution.py:335
  32.2 1.3 %shard_map.120.x_ref = bf16[512,640]{1,0:T(8,128)(2,1)S(1)} custom-call(bf16[20480,1024]{1,0:T(8,128)(2,1)} %shard_map.119.weights_hbm, bf16[32,32,640]{2,1,0:T(8,128)(2,1)S(1)} %all-to-all-done.recv_ref), custom_call_target="tpu_custom_call" | custom-call | flops 671088640 | bytes 1048576 | tf_op jit(solution)/shard_map/pallas_call | solution.py:358
  33.5 1.5 %collective-permute-start = (bf16[512,640]{1,0:T(8,128)(2,1)S(1)}, bf16[512,640]{1,0:T(8,128)(2,1)S(1)}, u32[]{:S(2)}, u32[]{:S(2)}) collective-permute-start(bf16[512,640]{1,0:T(8,128)(2,1)S(1)} %shard_map.120.x_ref), channel_id=1, source_target_pairs={{0,1},{1,2},{2,3},{3,0},{4,5},{5,6},{6,7},{7,4},{8,9},{9,10},{10,1... | collective-permute-start | bytes 1966088 | tf_op jit(solution)/shard_map/ppermute | solution.py:367
  35.0 0.0 collective-permute-done.1.half_hbm
  35.0 12.5 %shard_map.121 = (bf16[512,128]{1,0:T(8,128)(2,1)S(1)}, bf16[6,640,1024]{2,1,0:T(8,128)(2,1)S(1)}, bf16[64,6144]{1,0:T(8,128)(2,1)S(1)}) custom-call(bf16[512,640]{1,0:T(8,128)(2,1)S(1)} %shard_map.120.x_ref, bf16[1,6144]{1,0:T(2,128)(2,1)S(1)} %copy-done.2, f32[2,128]{1,0:T(2,128)S(1)} %bitcast.9, ...), custom_call_target="tpu_custom_call", output_to_operand_aliasing={{2}: (4, {})} | custom-call | flops 6442450944 | bytes 1048576 | tf_op jit(solution)/shard_map/pallas_call | solution.py:368
  47.4 2.3 %collective-permute-start.3 = (bf16[64,6144]{1,0:T(8,128)(2,1)S(1)}, bf16[64,6144]{1,0:T(8,128)(2,1)S(1)}, u32[]{:S(2)}, u32[]{:S(2)}) collective-permute-start(bf16[64,6144]{1,0:T(8,128)(2,1)S(1)} %get-tuple-element.16.mine_ref), channel_id=1, source_target_pairs={{0,4},{4,0},{8,12},{12,8},{16,20},{20,16},{24,28},{28,24},{32,36},... | collective-permute-start | bytes 2359304 | tf_op jit(solution)/shard_map/ppermute | solution.py:384
  49.7 1.2 %collective-permute-start.2 = (bf16[512,128]{1,0:T(8,128)(2,1)S(1)}, bf16[512,128]{1,0:T(8,128)(2,1)S(1)}, u32[]{:S(2)}, u32[]{:S(2)}) collective-permute-start(bf16[512,128]{1,0:T(8,128)(2,1)S(1)} %get-tuple-element.15), channel_id=1, source_target_pairs={{0,1},{1,2},{2,3},{3,0},{4,5},{5,6},{6,7},{7,4},{8,9},{9,10},{10,1... | collective-permute-start | bytes 393224 | tf_op jit(solution)/shard_map/ppermute | solution.py:383
  51.0 3.5 %shard_map.122.part_ref = f32[512,6144]{1,0:T(8,128)S(1)} custom-call(bf16[512,640]{1,0:T(8,128)(2,1)S(1)} %collective-permute-done.x_ref, bf16[6,640,1024]{2,1,0:T(8,128)(2,1)S(1)} %get-tuple-element.14.embed_ref), custom_call_target="tpu_custom_call" | custom-call | flops 4026531840 | bytes 1048576 | tf_op jit(solution)/shard_map/pallas_call | solution.py:386
  54.4 1.3 %collective-permute-done.2.attended_ref = bf16[512,128]{1,0:T(8,128)(2,1)S(1)} collective-permute-done((bf16[512,128]{1,0:T(8,128)(2,1)S(1)}, bf16[512,128]{1,0:T(8,128)(2,1)S(1)}, u32[]{:S(2)}, u32[]{:S(2)}) %collective-permute-start.2) | collective-permute-done | bytes 131104 | tf_op jit(solution)/shard_map/ppermute | solution.py:383
  55.7 3.2 %shard_map.123 = bf16[1,512,6144]{2,1,0:T(8,128)(2,1)} custom-call(f32[512,6144]{1,0:T(8,128)S(1)} %shard_map.122.part_ref, bf16[512,640]{1,0:T(8,128)(2,1)S(1)} %collective-permute-done.x_ref, bf16[512,128]{1,0:T(8,128)(2,1)S(1)} %collective-permute-done.2.attended_ref, bf16[6,640,1024]{2,1,0:T(8,128)(2,1)S(1)} %get-tuple-element.14.embed_ref, ...), custom_call_target="tpu_custom_call" | custom-call | flops 805306368 | bytes 1048576 | tf_op jit(solution)/shard_map/pallas_call | solution.py:395
  (13 shorter events, 0.0 us)
Async XLA Ops:
  3.3 9.8 %copy-start.7 = (bf16[64,6144]{1,0:T(8,128)(2,1)S(1)}, bf16[64,6144]{1,0:T(8,128)(2,1)}, u32[]{:S(2)}) copy-start(bf16[64,6144]{1,0:T(8,128)(2,1)} %get-tuple-element.13) | copy-start | bytes 2359300
  3.4 11.2 %slice-start = ((bf16[588,6144]{1,0:T(8,128)(2,1)}), bf16[12,6144]{1,0:T(8,128)(2,1)S(1)}, s32[]{:S(2)}) async-start(bf16[588,6144]{1,0:T(8,128)(2,1)} %embed_hbm.1), calls=%async_computation.1 | async-start | bytes 393216 | tf_op jit(solution)/shard_map/slice | solution.py:340
  3.4 11.2 %copy-start.5 = (bf16[8,6144]{1,0:T(8,128)(2,1)S(1)}, bf16[8,6144]{1,0:T(8,128)(2,1)}, u32[]{:S(2)}) copy-start(bf16[8,6144]{1,0:T(8,128)(2,1)} %param.19) | copy-start | bytes 294916
  3.4 11.2 %copy-start.6 = (bf16[8,6144]{1,0:T(8,128)(2,1)S(1)}, bf16[8,6144]{1,0:T(8,128)(2,1)}, u32[]{:S(2)}) copy-start(bf16[8,6144]{1,0:T(8,128)(2,1)} %param.18) | copy-start | bytes 294916
  3.4 11.3 %copy-start.3 = (f32[8,128]{1,0:T(8,128)S(1)}, f32[8,128]{1,0:T(8,128)}, u32[]{:S(2)}) copy-start(f32[8,128]{1,0:T(8,128)} %get-tuple-element.11.token_hbm) | copy-start | bytes 12292
  3.4 28.8 %all-to-all-start = ((bf16[32,32,640]{2,1,0:T(8,128)(2,1)}), bf16[32,32,640]{2,1,0:T(8,128)(2,1)S(1)}, u32[]{:S(2)}, u32[]{:S(2)}) async-start(bf16[32,32,640]{2,1,0:T(8,128)(2,1)} %get-tuple-element.12), calls=%async_computation | async-start | bytes 2621440 | tf_op jit(solution)/shard_map/all_to_all | solution.py:335
  13.2 21.8 %collective-permute-start.1 = (bf16[64,6144]{1,0:T(8,128)(2,1)S(1)}, bf16[64,6144]{1,0:T(8,128)(2,1)S(1)}, u32[]{:S(2)}, u32[]{:S(2)}) collective-permute-start(bf16[64,6144]{1,0:T(8,128)(2,1)S(1)} %copy-done.7), channel_id=1, source_target_pairs={{0,1},{1,2},{2,3},{3,0},{4,5},{5,6},{6,7},{7,4},{8,9},{9,10},{10,1... | collective-permute-start | bytes 2359304 | tf_op jit(solution)/shard_map/ppermute | solution.py:337
  14.7 3.1 %copy-start = (bf16[588,6144]{1,0:T(8,128)(2,1)S(1)}, bf16[588,6144]{1,0:T(8,128)(2,1)}, u32[]{:S(2)}) copy-start(bf16[588,6144]{1,0:T(8,128)(2,1)} %embed_hbm.1) | copy-start | bytes 21676036
  17.8 2.3 %copy-start.1 = (bf16[1,6144,384]{2,1,0:T(8,128)(2,1)S(1)}, bf16[1,6144,384]{2,1,0:T(8,128)(2,1)}, u32[]{:S(2)}) copy-start(bf16[1,6144,384]{2,1,0:T(8,128)(2,1)} %param.21) | copy-start | bytes 14155780
  26.2 8.7 %copy-start.2 = (bf16[1,6144]{1,0:T(2,128)(2,1)S(1)}, bf16[1,6144]{1,0:T(2,128)(2,1)}, u32[]{:S(2)}) copy-start(bf16[1,6144]{1,0:T(2,128)(2,1)} %gain_ref.1) | copy-start | bytes 36868
  26.3 8.7 %copy-start.4 = (f32[1,2,128]{2,1,0:T(2,128)S(1)}, f32[1,2,128]{2,1,0:T(2,128)}, u32[]{:S(2)}) copy-start(f32[1,2,128]{2,1,0:T(2,128)} %param.22) | copy-start | bytes 3076
  33.5 17.5 %collective-permute-start = (bf16[512,640]{1,0:T(8,128)(2,1)S(1)}, bf16[512,640]{1,0:T(8,128)(2,1)S(1)}, u32[]{:S(2)}, u32[]{:S(2)}) collective-permute-start(bf16[512,640]{1,0:T(8,128)(2,1)S(1)} %shard_map.120.x_ref), channel_id=1, source_target_pairs={{0,1},{1,2},{2,3},{3,0},{4,5},{5,6},{6,7},{7,4},{8,9},{9,10},{10,1... | collective-permute-start | bytes 1966088 | tf_op jit(solution)/shard_map/ppermute | solution.py:367
  47.4 8.3 %collective-permute-start.3 = (bf16[64,6144]{1,0:T(8,128)(2,1)S(1)}, bf16[64,6144]{1,0:T(8,128)(2,1)S(1)}, u32[]{:S(2)}, u32[]{:S(2)}) collective-permute-start(bf16[64,6144]{1,0:T(8,128)(2,1)S(1)} %get-tuple-element.16.mine_ref), channel_id=1, source_target_pairs={{0,4},{4,0},{8,12},{12,8},{16,20},{20,16},{24,28},{28,24},{32,36},... | collective-permute-start | bytes 2359304 | tf_op jit(solution)/shard_map/ppermute | solution.py:384
  49.7 6.0 %collective-permute-start.2 = (bf16[512,128]{1,0:T(8,128)(2,1)S(1)}, bf16[512,128]{1,0:T(8,128)(2,1)S(1)}, u32[]{:S(2)}, u32[]{:S(2)}) collective-permute-start(bf16[512,128]{1,0:T(8,128)(2,1)S(1)} %get-tuple-element.15), channel_id=1, source_target_pairs={{0,1},{1,2},{2,3},{3,0},{4,5},{5,6},{6,7},{7,4},{8,9},{9,10},{10,1... | collective-permute-start | bytes 393224 | tf_op jit(solution)/shard_map/ppermute | solution.py:383

commit v4 on v3

--- a/solution.py
+++ b/solution.py
@@ -34,8 +34,8 @@
 
 
 def pack_kernel(
-    shape_hbm, count_hbm, dest_hbm, keep_hbm, patches_hbm, weight_hbm, out_ref, half_ref, token_ref,
-    shape, count, dest, keep, patches, sems, patch_sems,
+    shape_hbm, count_hbm, dest_hbm, keep_hbm, patches_hbm, weight_hbm, out_ref, half_hbm, token_ref,
+    shape, count, dest, keep, patches, half, sems, patch_sems,
 ):
     images, patch_max, _ = patches.shape
     kept_max = keep.shape[1]
@@ -56,11 +56,12 @@
     for copy in small + large:
         copy.start()
     device = lax.axis_index("dp")
-    share = half_ref.shape[0]
-    half = pltpu.make_async_copy(
-        weight_hbm.at[pl.ds(pl.multiple_of(device % 2 * share, share), share)], half_ref, sems.at[4]
-    )
-    half.start()
+    share = half.shape[0]
+    half_in = pltpu.make_async_copy(
+        weight_hbm.at[pl.ds(pl.multiple_of(device % 2 * share, share), share)], half, sems.at[4]
+    )
+    half_out = pltpu.make_async_copy(half, half_hbm, sems.at[5])
+    half_in.start()
     out_ref[...] = jnp.zeros_like(out_ref)
     token_ref[...] = jnp.zeros_like(token_ref)
     number = iota((patch_max, 128), 0)
@@ -75,6 +76,8 @@
         flags[width] = ((lane == ROW_AT + row) | (lane == COL_AT + col) | source).astype(jnp.float32)
     for copy in small:
         copy.wait()
+    unit = as_bf16(iota((images, images), 0) == iota((images, images), 1))
+    listed = dot(keep[...].astype(jnp.float32).astype(jnp.bfloat16), unit, ((0,), (0,))).astype(jnp.int32)
     for g in range(images):
         if g % step == 0:
             large[g // step].wait()
@@ -82,19 +85,23 @@
         own = flags[SIDE_MAX]
         for side in range(SIDE_MIN, SIDE_MAX):
             own = jnp.where(width == side, flags[side], own)
-        picked = (iota((patch_max, kept_max), 0) == keep[g : g + 1, :]) & (
-            iota((patch_max, kept_max), 1) < count[0, g]
+        picked = (iota((kept_max, patch_max), 1) == listed[:, g : g + 1]) & (
+            iota((kept_max, patch_max), 0) < count[0, g]
         )
         picked = as_bf16(picked)
         there = dest[0, g]
-        body = dot(picked, patches[g, :, :TAIL], ((0,), (0,)))
-        out_ref[there, :, :TAIL] = body.astype(jnp.bfloat16)
+        out_ref[there, :, :TAIL] = dot(picked, patches[g, :, :TAIL]).astype(jnp.bfloat16)
         last = jnp.concatenate([patches[g, :, TAIL:], own.astype(jnp.bfloat16)[:, ROW_AT:]], axis=1)
-        out_ref[there, :, TAIL:] = dot(picked, last, ((0,), (0,))).astype(jnp.bfloat16)
-    half.wait()
-
-
-def compact_kernel(weights_hbm, recv_ref, out_ref):
+        out_ref[there, :, TAIL:] = dot(picked, last).astype(jnp.bfloat16)
+        if g == images // 2:
+            half_in.wait()
+            half_out.start()
+    half_out.wait()
+
+
+def compact_kernel(weights_hbm, recv_ref, out_ref, early_ref, sems):
+    (early,) = tile_copies(weights_hbm, 1, early_ref, sems)
+    early.start()
     sources, kept_max, lanes = recv_ref.shape
     total = sources * kept_max
     blocks = total // 128
@@ -117,6 +124,7 @@
     slot = iota((seq_len, 128), 0)
     hot = jnp.concatenate([as_bf16(slot == place[b : b + 1, :]) for b in range(blocks)], axis=1)
     out_ref[...] = dot(hot, received).astype(jnp.bfloat16)
+    early.wait()
 
 
 def lane_sums(values, sums):
@@ -131,78 +139,82 @@
     return (centre * lax.rsqrt(spread + eps) * gain).astype(jnp.bfloat16)
 
 
-def weight_kernel(token_hbm, embed_hbm, tail_hbm, qkv_hbm, out_hbm, embed, qkv, sems, out_sems):
-    tiles, lanes, _ = embed.shape
-    depth = lanes - tail_hbm.shape[0]
-    copies, results = [], []
+def weight_kernel(token_hbm, embed_ref, tail_ref, qkv_ref, out_hbm, tile_ref, sems):
+    tail = tail_ref.shape[0]
+    depth = LANES - tail
+    tiles = embed_ref.shape[1] // TILE
+    copies = []
     for t in range(tiles):
         columns = pl.ds(t * TILE, TILE)
+        for source, first, rows in ((embed_ref, t * LANES, depth), (tail_ref, t * LANES + depth, tail)):
+            copies.append(
+                pltpu.make_async_copy(
+                    source.at[pl.ds(0, rows), columns], out_hbm.at[pl.ds(first, rows)], sems.at[len(copies)]
+                )
+            )
+    columns = pl.ds(0, TILE)
+    for source, first, rows in ((embed_ref, 0, depth), (tail_ref, depth, tail)):
         copies.append(
-            (
-                pltpu.make_async_copy(
-                    embed_hbm.at[pl.ds(0, depth), columns], embed.at[t, pl.ds(0, depth)], sems.at[2 * t]
-                ),
-                pltpu.make_async_copy(
-                    tail_hbm.at[:, columns],
-                    embed.at[t, pl.ds(depth, tail_hbm.shape[0])],
-                    sems.at[2 * t + 1],
-                ),
+            pltpu.make_async_copy(
+                source.at[pl.ds(0, rows), columns],
+                tile_ref.at[0, pl.ds(first, rows)],
+                sems.at[len(copies)],
             )
         )
-        results.append(
-            pltpu.make_async_copy(embed.at[t], out_hbm.at[pl.ds(t * lanes, lanes)], out_sems.at[t])
-        )
-    copies.append((pltpu.make_async_copy(qkv_hbm, qkv, sems.at[2 * tiles]),))
-    results.append(pltpu.make_async_copy(qkv, qkv_part(out_hbm, tiles * lanes, qkv), out_sems.at[tiles]))
-    for pair in copies:
-        for copy in pair:
-            copy.start()
-    for pair, result in zip(copies, results):
-        for copy in pair:
-            copy.wait()
-        result.start()
-    for result in results:
-        result.wait()
+    copies.append(
+        pltpu.make_async_copy(qkv_ref, qkv_part(out_hbm, tiles * LANES, qkv_ref), sems.at[len(copies)])
+    )
+    for copy in copies:
+        copy.start()
+    for copy in copies:
+        copy.wait()
 
 
 def qkv_part(weights, first, qkv):
     return weights.at[pl.ds(first, qkv.shape[0]), pl.ds(0, qkv.shape[1])]
 
 
-def tile_copies(weights_hbm, embed, sems):
+def tile_copies(weights_hbm, first, embed, sems):
     tiles, lanes, _ = embed.shape
     return [
-        pltpu.make_async_copy(weights_hbm.at[pl.ds(t * lanes, lanes)], embed.at[t], sems.at[t])
+        pltpu.make_async_copy(weights_hbm.at[pl.ds((first + t) * lanes, lanes)], embed.at[t], sems.at[t])
         for t in range(tiles)
     ]
 
 
+def hand_on_kernel(token_hbm, half_hbm, same_half_hbm):
+    pass
+
+
 def attend_kernel(
-    x_ref, gain_ref, norm_ref, weights_hbm, half_hbm,
-    out_ref, embed, same_half_hbm, tokens, qkv, sems, qkv_sem,
+    x_ref, gain_ref, norm_ref, tile_ref, early_ref, weights_hbm, out_ref, late_ref, token_ref,
+    tokens, qkv, sems, qkv_sem,
 ):
-    tiles, lanes, _ = embed.shape
-    copies = tile_copies(weights_hbm, embed, sems)
-    qkv_copy = pltpu.make_async_copy(qkv_part(weights_hbm, tiles * lanes, qkv), qkv, qkv_sem.at[0])
-    width = tiles * TILE
+    late, lanes, _ = late_ref.shape
+    copies = tile_copies(weights_hbm, 2, late_ref, sems)
+    qkv_copy = pltpu.make_async_copy(qkv_part(weights_hbm, (2 + late) * lanes, qkv), qkv, qkv_sem.at[0])
+    width = (2 + late) * TILE
     copies[0].start()
     copies[1].start()
+    token_ref[...] = jnp.zeros_like(token_ref)
     x = x_ref[...]
     rows = x.shape[0]
     spans = [slice(at, at + TILE) for at in range(0, width, TILE)]
     total = jnp.zeros((rows, 128), jnp.float32)
     squares = jnp.zeros((rows, 128), jnp.float32)
     for t, span in enumerate(spans):
-        if t < 2:
-            copies[t].wait()
-            for later in copies[2 * t + 2 : 2 * t + 4]:
-                later.start()
-        elif t % 2 == 0:
-            copies[t].wait()
-            copies[t + 1].wait()
-            if t == 2:
-                qkv_copy.start()
-        part = dot(x, embed[t]).astype(jnp.bfloat16)
+        if t == 1:
+            copies[2].start()
+            copies[3].start()
+        if t == 2:
+            copies[0].wait()
+            copies[1].wait()
+            qkv_copy.start()
+        if t == 4:
+            copies[2].wait()
+            copies[3].wait()
+        tile = (tile_ref[0], early_ref[0])[t] if t < 2 else late_ref[t - 2]
+        part = dot(x, tile).astype(jnp.bfloat16)
         tokens[:, span] = part
         part = part.astype(jnp.float32)
         total = lane_sums(part, total)
@@ -238,14 +250,18 @@
         out_ref[here, :] = attended.astype(jnp.bfloat16)
 
 
-def embed_kernel(x_ref, embed_ref, out_ref):
-    for t in range(embed_ref.shape[0]):
+def embed_kernel(x_ref, tile_ref, early_ref, late_ref, half_hbm, out_ref, half_ref, sem):
+    copy = pltpu.make_async_copy(half_hbm, half_ref, sem.at[0])
+    copy.start()
+    for t in range(2 + late_ref.shape[0]):
         span = slice(t * TILE, (t + 1) * TILE)
-        out_ref[:, span] = dot(x_ref[:, :TAIL], embed_ref[t, :TAIL])
+        tile = (tile_ref[0, :TAIL], early_ref[0, :TAIL])[t] if t < 2 else late_ref[t - 2, :TAIL]
+        out_ref[:, span] = dot(x_ref[:, :TAIL], tile)
+    copy.wait()
 
 
 def section_kernel(
-    part_ref, x_ref, attended_ref, embed_ref, mine_ref, other_ref, out_hbm, weight, out, sems
+    part_ref, x_ref, attended_ref, tile_ref, early_ref, late_ref, mine_ref, other_ref, out_hbm, weight, out, sems
 ):
     half = mine_ref.shape[0]
     last = x_ref.shape[1] - TAIL
@@ -256,7 +272,8 @@
     results = []
     for t in range(out.shape[1] // TILE):
         span = slice(t * TILE, (t + 1) * TILE)
-        weight[:last, span] = embed_ref[t, TAIL:]
+        tile = (tile_ref[0, TAIL:], early_ref[0, TAIL:])[t] if t < 2 else late_ref[t - 2, TAIL:]
+        weight[:last, span] = tile
         out[:, span] = (part_ref[:, span] + dot(both, weight[:, span])).astype(jnp.bfloat16)
         columns = pl.ds(t * TILE, TILE)
         result = pltpu.make_async_copy(out.at[:, columns], out_hbm.at[0, :, columns], sems.at[t])
@@ -319,14 +336,15 @@
         pack_kernel,
         [bf16(groups, kept_max, LANES), bf16(head // 2, width), token],
         [HBM] * 6,
-        [VMEM] * 3,
+        [VMEM, HBM, VMEM],
         [
             pltpu.SMEM((2, images), jnp.int32),
             pltpu.SMEM((1, images), jnp.int32),
             pltpu.SMEM((1, images), jnp.int32),
             pltpu.VMEM((images, kept_max), jnp.int32),
             pltpu.VMEM((images, patch_max, patch_width), jnp.bfloat16),
-            dma((5,)),
+            pltpu.VMEM((head // 2, width), jnp.bfloat16),
+            dma((6,)),
             dma((parts,)),
         ],
         60,
@@ -344,67 +362,67 @@
         ],
         axis=0,
     )
-    embed_scratch = pltpu.VMEM((tiles, LANES, TILE), jnp.bfloat16)
-    qkv_scratch = pltpu.VMEM((width, 3 * head), jnp.bfloat16)
-    weights = call(
+    weights, tile = call(
         weight_kernel,
-        bf16(STORE, TILE),
-        [HBM] * 4,
-        HBM,
-        [embed_scratch, qkv_scratch, dma((2 * tiles + 1,)), dma((tiles + 1,))],
+        [bf16(STORE, TILE), bf16(1, LANES, TILE)],
+        [HBM] + [VMEM] * 3,
+        [HBM, VMEM],
+        [dma((2 * tiles + 3,))],
         20,
         MIB,
     )(after_pack, embed_weight, tail, qkv_weight[0])
-    x = call(
+    x, early = call(
         compact_kernel,
-        bf16(seq_len, LANES),
+        [bf16(seq_len, LANES), bf16(1, LANES, TILE)],
         [HBM, VMEM],
-        VMEM,
-        [],
+        [VMEM] * 2,
+        [dma((1,))],
         16,
         2 * seq_len * groups * kept_max * LANES,
     )(weights, received)
     next_x = lax.ppermute(x, "segment", onward)
-    attended, embed, half = call(
+    attended, late, after_attend = call(
         attend_kernel,
-        [bf16(seq_len, head), bf16(tiles, LANES, TILE), bf16(head // 2, width)],
-        [VMEM] * 3 + [HBM] * 2,
-        [VMEM, VMEM, HBM],
+        [bf16(seq_len, head), bf16(tiles - 2, LANES, TILE), token],
+        [VMEM] * 5 + [HBM],
+        [VMEM] * 3,
         [
             pltpu.VMEM((seq_len, width), jnp.bfloat16),
-            qkv_scratch,
-            dma((tiles,)),
+            pltpu.VMEM((width, 3 * head), jnp.bfloat16),
+            dma((tiles - 2,)),
             dma((1,)),
         ],
         34,
         2 * seq_len * width * (LANES + 3 * head),
-        {4: 2},
-    )(x, ln_gain, norm_gains[0], weights, half)
+    )(x, ln_gain, norm_gains[0], tile, early, weights)
     next_attended = lax.ppermute(attended, "segment", onward)
+    half = call(hand_on_kernel, bf16(head // 2, width), [HBM, HBM], HBM, [], 4, MIB, {1: 0})(
+        after_attend, half
+    )
     other = lax.ppermute(half, "dp", pairs)
 
-    part = call(
+    part, half = call(
         embed_kernel,
-        jax.ShapeDtypeStruct((seq_len, width), jnp.float32),
+        [jax.ShapeDtypeStruct((seq_len, width), jnp.float32), bf16(head // 2, width)],
+        [VMEM] * 4 + [HBM],
         [VMEM] * 2,
-        VMEM,
-        [],
-        24,
+        [dma((1,))],
+        16,
         2 * seq_len * width * LANES,
-    )(next_x, embed)
+    )(next_x, tile, early, late, half)
     return call(
         section_kernel,
         bf16(1, seq_len, width),
-        [VMEM] * 6,
+        [VMEM] * 8,
         HBM,
         [
             pltpu.VMEM((LANES - TAIL + head, width), jnp.bfloat16),
             pltpu.VMEM((seq_len, width), jnp.bfloat16),
             dma((tiles,)),
         ],
-        30,
+        20,
         2 * seq_len * width * head,
-    )(part, next_x, next_attended, embed, half, other)
+    )(part, next_x, next_attended, tile, early, late, half, other)
 
 
 def solution(mesh):

time: 59.5 us -> 59.1 us (level)
  Pallas kernels: 29.8 us -> 27.5 us
  waiting for transfers between devices: 7.29 us -> 8.72 us
    pallas_call x5 -> x6, Pallas kernels: 26.5 us -> 23.7 us  [the longest x1 11 us: shards(): call(attend_kernel, [bf16(seq_len, head), bf16(tiles - 2, LANES, TILE), t...]
    all_to_all x1, waiting for transfers between devices: 5.97 us -> 7.44 us  [shards(): lax.all_to_all(packed, 'dp', split_axis=0, concat_axis=0, tiled=True)]
    unnamed x16 -> x14, local copies, waits for them, and re-layouts: 5.43 us -> 5.42 us
  transfers between devices with their start and end apart: 5 -> 5, of which waited for: 2 -> 2; matrix products, arithmetic and copies ran while one was open for 0% -> 0% of each run, Pallas kernels for 39% -> 35%
where the time goes in v4:
time: 59.1 us; the launch traced here: 58.2 us
  Pallas kernels  27.5 us (47%)
  starting transfers between devices  16 us (27%)
  waiting for transfers between devices  8.72 us (15%)
  local copies, waits for them, and re-layouts  5.51 us (9%)
    pallas_call x1, Pallas kernels, shards(): call(attend_kernel, [bf16(seq_len, head), bf16(tiles - 2, LANES, TILE), t...  11 us
    all_to_all x1, starting transfers between devices, shards(): lax.all_to_all(packed, 'dp', split_axis=0, concat_axis=0, tiled=True)  9.74 us
    all_to_all x1, waiting for transfers between devices, shards(): lax.all_to_all(packed, 'dp', split_axis=0, concat_axis=0, tiled=True)  7.44 us
    unnamed x14, local copies, waits for them, and re-layouts  5.42 us
    pallas_call x1, Pallas kernels, shards(): call(weight_kernel, [bf16(STORE, TILE), bf16(1, LANES, TILE)], [HBM] + [V...  4.69 us
    pallas_call x1, Pallas kernels, shards(): call(pack_kernel, [bf16(groups, kept_max, LANES), bf16(head // 2, width),...  3.8 us
    pallas_call x1, Pallas kernels, shards(): call(embed_kernel, [jax.ShapeDtypeStruct((seq_len, width), jnp.float32),...  3.5 us
    pallas_call x1, Pallas kernels, shards(): call(section_kernel, bf16(1, seq_len, width), [VMEM] * 8, HBM, [pltpu.VME...  3.19 us
  transfers between devices with their start and end apart: 5, of which 2 were waited for; matrix products, arithmetic and copies ran while one was open for 0% of the time, Pallas kernels for 35%

profile of v4, /device:TPU:1, one launch (start us, length us, event | category | flops | bytes accessed | tf_op | source)
XLA Modules:
  0.0 58.2 jit_solution(4840757537243892873)
XLA Ops:
  0.0 3.8 %shard_map.118 = (bf16[32,32,640]{2,1,0:T(8,128)(2,1)}, bf16[64,6144]{1,0:T(8,128)(2,1)}, f32[8,128]{1,0:T(8,128)}) custom-call(s32[2,16]{1,0:T(2,128)} %bitcast.13, s32[1,16]{1,0:T(1,128)} %count_hbm.1, s32[1,16]{1,0:T(1,128)} %dest_hbm.1, s32[16,32]{1,0:T(8,128)} %bitcast.12, bf16[16,64,588]{2,1,0:T(8,128)(2,1)} %bitcast.11, bf16[128,6144]{1,0:T(8,128)(2,1)} %bitcast.10), custom_call_target="tpu_custom_call" | custom-call | flops 41943040 | bytes 1048576 | tf_op jit(solution)/shard_map/pallas_call | solution.py:335
  3.8 0.0 slice-start
  3.8 0.0 copy-start.5
  3.8 0.0 copy-start.6
  3.9 9.7 %all-to-all-start = ((bf16[32,32,640]{2,1,0:T(8,128)(2,1)}), bf16[32,32,640]{2,1,0:T(8,128)(2,1)S(1)}, u32[]{:S(2)}, u32[]{:S(2)}) async-start(bf16[32,32,640]{2,1,0:T(8,128)(2,1)} %get-tuple-element.19), calls=%async_computation | async-start | bytes 2621440 | tf_op jit(solution)/shard_map/all_to_all | solution.py:353
  13.6 1.3 %collective-permute-start.1 = (bf16[64,6144]{1,0:T(8,128)(2,1)}, bf16[64,6144]{1,0:T(8,128)(2,1)S(1)}, u32[]{:S(2)}, u32[]{:S(2)}) collective-permute-start(bf16[64,6144]{1,0:T(8,128)(2,1)} %get-tuple-element.25), channel_id=1, source_target_pairs={{0,1},{1,2},{2,3},{3,0},{4,5},{5,6},{6,7},{7,4},{8,9},{9,10},{10,1... | collective-permute-start | bytes 2359304 | tf_op jit(solution)/shard_map/ppermute | solution.py:355
  14.9 0.1 pad.3.clone
  15.0 0.2 maximum_maximum_fusion.tail_ref
  15.2 0.0 copy-start
  15.2 3.1 %copy-done = bf16[588,6144]{1,0:T(8,128)(2,1)S(1)} copy-done((bf16[588,6144]{1,0:T(8,128)(2,1)S(1)}, bf16[588,6144]{1,0:T(8,128)(2,1)}, u32[]{:S(2)}) %copy-start) | copy-done | bytes 7225368
  18.2 2.3 %copy-done.1 = bf16[1,6144,384]{2,1,0:T(8,128)(2,1)S(1)} copy-done((bf16[1,6144,384]{2,1,0:T(8,128)(2,1)S(1)}, bf16[1,6144,384]{2,1,0:T(8,128)(2,1)}, u32[]{:S(2)}) %copy-start.1) | copy-done | bytes 4718616
  20.6 4.7 %shard_map.119 = (bf16[20480,1024]{1,0:T(8,128)(2,1)}, bf16[1,640,1024]{2,1,0:T(8,128)(2,1)S(1)}) custom-call(f32[8,128]{1,0:T(8,128)S(1)} %copy-done.3, bf16[588,6144]{1,0:T(8,128)(2,1)S(1)} %copy-done, bf16[64,6144]{1,0:T(8,128)(2,1)S(1)} %maximum_maximum_fusion.tail_ref, bf16[6144,384]{1,0:T(8,128)(2,1)S(1)} %bitcast.8), custom_call_target="tpu_custom_call" | custom-call | flops 1048576 | bytes 1048576 | tf_op jit(solution)/shard_map/pallas_call | solution.py:365
  25.3 7.4 %all-to-all-done.recv_ref = bf16[32,32,640]{2,1,0:T(8,128)(2,1)S(1)} async-done(((bf16[32,32,640]{2,1,0:T(8,128)(2,1)}), bf16[32,32,640]{2,1,0:T(8,128)(2,1)S(1)}, u32[]{:S(2)}, u32[]{:S(2)}) %all-to-all-start) | async-done | bytes 1310752 | tf_op jit(solution)/shard_map/all_to_all | solution.py:353
  32.7 1.4 %shard_map.120 = (bf16[512,640]{1,0:T(8,128)(2,1)S(1)}, bf16[1,640,1024]{2,1,0:T(8,128)(2,1)S(1)}) custom-call(bf16[20480,1024]{1,0:T(8,128)(2,1)} %get-tuple-element.18.weights_hbm, bf16[32,32,640]{2,1,0:T(8,128)(2,1)S(1)} %all-to-all-done.recv_ref), custom_call_target="tpu_custom_call" | custom-call | flops 671088640 | bytes 1048576 | tf_op jit(solution)/shard_map/pallas_call | solution.py:374
  34.1 1.5 %collective-permute-start = (bf16[512,640]{1,0:T(8,128)(2,1)S(1)}, bf16[512,640]{1,0:T(8,128)(2,1)S(1)}, u32[]{:S(2)}, u32[]{:S(2)}) collective-permute-start(bf16[512,640]{1,0:T(8,128)(2,1)S(1)} %get-tuple-element.20.x_ref), channel_id=1, source_target_pairs={{0,1},{1,2},{2,3},{3,0},{4,5},{5,6},{6,7},{7,4},{8,9},{9,10},{10,1... | collective-permute-start | bytes 1966088 | tf_op jit(solution)/shard_map/ppermute | solution.py:383
  35.5 11.0 %shard_map.121 = (bf16[512,128]{1,0:T(8,128)(2,1)S(1)}, bf16[4,640,1024]{2,1,0:T(8,128)(2,1)S(1)}, f32[8,128]{1,0:T(8,128)S(1)}) custom-call(bf16[512,640]{1,0:T(8,128)(2,1)S(1)} %get-tuple-element.20.x_ref, bf16[1,6144]{1,0:T(2,128)(2,1)S(1)} %copy-done.2, f32[2,128]{1,0:T(2,128)S(1)} %bitcast.9, bf16[1,640,1024]{2,1,0:T(8,128)(2,1)S(1)} %get-tuple-element.21.tile_ref, ...), custom_call_target="tpu_custom_call" | custom-call | flops 6442450944 | bytes 1048576 | tf_op jit(solution)/shard_map/pallas_call | solution.py:384
  46.5 0.0 collective-permute-done.1.half_hbm
  46.5 2.3 %collective-permute-start.3 = (bf16[64,6144]{1,0:T(8,128)(2,1)S(1)}, bf16[64,6144]{1,0:T(8,128)(2,1)S(1)}, u32[]{:S(2)}, u32[]{:S(2)}) collective-permute-start(bf16[64,6144]{1,0:T(8,128)(2,1)S(1)} %shard_map.122.half_hbm), channel_id=1, source_target_pairs={{0,4},{4,0},{8,12},{12,8},{16,20},{20,16},{24,28},{28,24},{32,36},... | collective-permute-start | bytes 2359304 | tf_op jit(solution)/shard_map/ppermute | solution.py:402
  48.8 1.2 %collective-permute-start.2 = (bf16[512,128]{1,0:T(8,128)(2,1)S(1)}, bf16[512,128]{1,0:T(8,128)(2,1)S(1)}, u32[]{:S(2)}, u32[]{:S(2)}) collective-permute-start(bf16[512,128]{1,0:T(8,128)(2,1)S(1)} %get-tuple-element.27), channel_id=1, source_target_pairs={{0,1},{1,2},{2,3},{3,0},{4,5},{5,6},{6,7},{7,4},{8,9},{9,10},{10,1... | collective-permute-start | bytes 393224 | tf_op jit(solution)/shard_map/ppermute | solution.py:398
  50.0 0.0 collective-permute-done.x_ref
  50.0 3.5 %shard_map.123 = (f32[512,6144]{1,0:T(8,128)S(1)}, bf16[64,6144]{1,0:T(8,128)(2,1)S(1)}) custom-call(bf16[512,640]{1,0:T(8,128)(2,1)S(1)} %collective-permute-done.x_ref, bf16[1,640,1024]{2,1,0:T(8,128)(2,1)S(1)} %get-tuple-element.21.tile_ref, bf16[1,640,1024]{2,1,0:T(8,128)(2,1)S(1)} %get-tuple-element.22.early_ref, ...), custom_call_target="tpu_custom_call" | custom-call | flops 4026531840 | bytes 1048576 | tf_op jit(solution)/shard_map/pallas_call | solution.py:404
  53.5 1.3 %collective-permute-done.2.attended_ref = bf16[512,128]{1,0:T(8,128)(2,1)S(1)} collective-permute-done((bf16[512,128]{1,0:T(8,128)(2,1)S(1)}, bf16[512,128]{1,0:T(8,128)(2,1)S(1)}, u32[]{:S(2)}, u32[]{:S(2)}) %collective-permute-start.2) | collective-permute-done | bytes 131104 | tf_op jit(solution)/shard_map/ppermute | solution.py:398
  54.8 0.0 collective-permute-done.3.other_ref
  54.8 3.2 %shard_map.124 = bf16[1,512,6144]{2,1,0:T(8,128)(2,1)} custom-call(f32[512,6144]{1,0:T(8,128)S(1)} %get-tuple-element.26.part_ref, bf16[512,640]{1,0:T(8,128)(2,1)S(1)} %collective-permute-done.x_ref, bf16[512,128]{1,0:T(8,128)(2,1)S(1)} %collective-permute-done.2.attended_ref, bf16[1,640,1024]{2,1,0:T(8,128)(2,1)S(1)} %get-tuple-element.21.tile_ref, ...), custom_call_target="tpu_custom_call" | custom-call | flops 805306368 | bytes 1048576 | tf_op jit(solution)/shard_map/pallas_call | solution.py:413
  (12 shorter events, 0.0 us)
Async XLA Ops:
  3.8 11.2 %slice-start = ((bf16[588,6144]{1,0:T(8,128)(2,1)}), bf16[12,6144]{1,0:T(8,128)(2,1)S(1)}, s32[]{:S(2)}) async-start(bf16[588,6144]{1,0:T(8,128)(2,1)} %embed_ref.1), calls=%async_computation.1 | async-start | bytes 393216 | tf_op jit(solution)/shard_map/slice | solution.py:358
  3.8 11.2 %copy-start.5 = (bf16[8,6144]{1,0:T(8,128)(2,1)S(1)}, bf16[8,6144]{1,0:T(8,128)(2,1)}, u32[]{:S(2)}) copy-start(bf16[8,6144]{1,0:T(8,128)(2,1)} %param.19) | copy-start | bytes 294916
  3.8 11.1 %copy-start.6 = (bf16[8,6144]{1,0:T(8,128)(2,1)S(1)}, bf16[8,6144]{1,0:T(8,128)(2,1)}, u32[]{:S(2)}) copy-start(bf16[8,6144]{1,0:T(8,128)(2,1)} %param.18) | copy-start | bytes 294916
  3.8 11.3 %copy-start.3 = (f32[8,128]{1,0:T(8,128)S(1)}, f32[8,128]{1,0:T(8,128)}, u32[]{:S(2)}) copy-start(f32[8,128]{1,0:T(8,128)} %get-tuple-element.17.token_hbm) | copy-start | bytes 12292
  3.9 28.8 %all-to-all-start = ((bf16[32,32,640]{2,1,0:T(8,128)(2,1)}), bf16[32,32,640]{2,1,0:T(8,128)(2,1)S(1)}, u32[]{:S(2)}, u32[]{:S(2)}) async-start(bf16[32,32,640]{2,1,0:T(8,128)(2,1)} %get-tuple-element.19), calls=%async_computation | async-start | bytes 2621440 | tf_op jit(solution)/shard_map/all_to_all | solution.py:353
  13.6 32.9 %collective-permute-start.1 = (bf16[64,6144]{1,0:T(8,128)(2,1)}, bf16[64,6144]{1,0:T(8,128)(2,1)S(1)}, u32[]{:S(2)}, u32[]{:S(2)}) collective-permute-start(bf16[64,6144]{1,0:T(8,128)(2,1)} %get-tuple-element.25), channel_id=1, source_target_pairs={{0,1},{1,2},{2,3},{3,0},{4,5},{5,6},{6,7},{7,4},{8,9},{9,10},{10,1... | collective-permute-start | bytes 2359304 | tf_op jit(solution)/shard_map/ppermute | solution.py:355
  15.2 3.1 %copy-start = (bf16[588,6144]{1,0:T(8,128)(2,1)S(1)}, bf16[588,6144]{1,0:T(8,128)(2,1)}, u32[]{:S(2)}) copy-start(bf16[588,6144]{1,0:T(8,128)(2,1)} %embed_ref.1) | copy-start | bytes 21676036
  18.2 2.3 %copy-start.1 = (bf16[1,6144,384]{2,1,0:T(8,128)(2,1)S(1)}, bf16[1,6144,384]{2,1,0:T(8,128)(2,1)}, u32[]{:S(2)}) copy-start(bf16[1,6144,384]{2,1,0:T(8,128)(2,1)} %param.21) | copy-start | bytes 14155780
  32.7 2.8 %copy-start.2 = (bf16[1,6144]{1,0:T(2,128)(2,1)S(1)}, bf16[1,6144]{1,0:T(2,128)(2,1)}, u32[]{:S(2)}) copy-start(bf16[1,6144]{1,0:T(2,128)(2,1)} %gain_ref.1) | copy-start | bytes 36868
  32.7 2.8 %copy-start.4 = (f32[1,2,128]{2,1,0:T(2,128)S(1)}, f32[1,2,128]{2,1,0:T(2,128)}, u32[]{:S(2)}) copy-start(f32[1,2,128]{2,1,0:T(2,128)} %param.22) | copy-start | bytes 3076
  34.1 16.0 %collective-permute-start = (bf16[512,640]{1,0:T(8,128)(2,1)S(1)}, bf16[512,640]{1,0:T(8,128)(2,1)S(1)}, u32[]{:S(2)}, u32[]{:S(2)}) collective-permute-start(bf16[512,640]{1,0:T(8,128)(2,1)S(1)} %get-tuple-element.20.x_ref), channel_id=1, source_target_pairs={{0,1},{1,2},{2,3},{3,0},{4,5},{5,6},{6,7},{7,4},{8,9},{9,10},{10,1... | collective-permute-start | bytes 1966088 | tf_op jit(solution)/shard_map/ppermute | solution.py:383
  46.5 8.3 %collective-permute-start.3 = (bf16[64,6144]{1,0:T(8,128)(2,1)S(1)}, bf16[64,6144]{1,0:T(8,128)(2,1)S(1)}, u32[]{:S(2)}, u32[]{:S(2)}) collective-permute-start(bf16[64,6144]{1,0:T(8,128)(2,1)S(1)} %shard_map.122.half_hbm), channel_id=1, source_target_pairs={{0,4},{4,0},{8,12},{12,8},{16,20},{20,16},{24,28},{28,24},{32,36},... | collective-permute-start | bytes 2359304 | tf_op jit(solution)/shard_map/ppermute | solution.py:402
  48.8 6.0 %collective-permute-start.2 = (bf16[512,128]{1,0:T(8,128)(2,1)S(1)}, bf16[512,128]{1,0:T(8,128)(2,1)S(1)}, u32[]{:S(2)}, u32[]{:S(2)}) collective-permute-start(bf16[512,128]{1,0:T(8,128)(2,1)S(1)} %get-tuple-element.27), channel_id=1, source_target_pairs={{0,1},{1,2},{2,3},{3,0},{4,5},{5,6},{6,7},{7,4},{8,9},{9,10},{10,1... | collective-permute-start | bytes 393224 | tf_op jit(solution)/shard_map/ppermute | solution.py:398

commit v5 on v4

--- a/solution.py
+++ b/solution.py
@@ -34,8 +34,8 @@
 
 
 def pack_kernel(
-    shape_hbm, count_hbm, dest_hbm, keep_hbm, patches_hbm, weight_hbm, out_ref, half_hbm, token_ref,
-    shape, count, dest, keep, patches, half, sems, patch_sems,
+    shape_hbm, count_hbm, dest_hbm, keep_hbm, patches_hbm, weight_hbm, out_ref, half_ref, token_ref,
+    shape, count, dest, keep, patches, sems, patch_sems,
 ):
     images, patch_max, _ = patches.shape
     kept_max = keep.shape[1]
@@ -56,12 +56,11 @@
     for copy in small + large:
         copy.start()
     device = lax.axis_index("dp")
-    share = half.shape[0]
-    half_in = pltpu.make_async_copy(
-        weight_hbm.at[pl.ds(pl.multiple_of(device % 2 * share, share), share)], half, sems.at[4]
-    )
-    half_out = pltpu.make_async_copy(half, half_hbm, sems.at[5])
-    half_in.start()
+    share = half_ref.shape[0]
+    half = pltpu.make_async_copy(
+        weight_hbm.at[pl.ds(pl.multiple_of(device % 2 * share, share), share)], half_ref, sems.at[4]
+    )
+    half.start()
     out_ref[...] = jnp.zeros_like(out_ref)
     token_ref[...] = jnp.zeros_like(token_ref)
     number = iota((patch_max, 128), 0)
@@ -76,8 +75,6 @@
         flags[width] = ((lane == ROW_AT + row) | (lane == COL_AT + col) | source).astype(jnp.float32)
     for copy in small:
         copy.wait()
-    unit = as_bf16(iota((images, images), 0) == iota((images, images), 1))
-    listed = dot(keep[...].astype(jnp.float32).astype(jnp.bfloat16), unit, ((0,), (0,))).astype(jnp.int32)
     for g in range(images):
         if g % step == 0:
             large[g // step].wait()
@@ -85,18 +82,16 @@
         own = flags[SIDE_MAX]
         for side in range(SIDE_MIN, SIDE_MAX):
             own = jnp.where(width == side, flags[side], own)
-        picked = (iota((kept_max, patch_max), 1) == listed[:, g : g + 1]) & (
-            iota((kept_max, patch_max), 0) < count[0, g]
+        picked = (iota((patch_max, kept_max), 0) == keep[g : g + 1, :]) & (
+            iota((patch_max, kept_max), 1) < count[0, g]
         )
         picked = as_bf16(picked)
         there = dest[0, g]
-        out_ref[there, :, :TAIL] = dot(picked, patches[g, :, :TAIL]).astype(jnp.bfloat16)
+        body = dot(picked, patches[g, :, :TAIL], ((0,), (0,)))
+        out_ref[there, :, :TAIL] = body.astype(jnp.bfloat16)
         last = jnp.concatenate([patches[g, :, TAIL:], own.astype(jnp.bfloat16)[:, ROW_AT:]], axis=1)
-        out_ref[there, :, TAIL:] = dot(picked, last).astype(jnp.bfloat16)
-        if g == images // 2:
-            half_in.wait()
-            half_out.start()
-    half_out.wait()
+        out_ref[there, :, TAIL:] = dot(picked, last, ((0,), (0,))).astype(jnp.bfloat16)
+    half.wait()
 
 
 def compact_kernel(weights_hbm, recv_ref, out_ref, early_ref, sems):
@@ -326,7 +321,7 @@
     width = embed_weight.shape[1]
     head = out_weight.shape[1]
     tiles = width // TILE
-    parts = 4
+    parts = 1
     onward = [(source, (source + 1) % segments) for source in range(segments)]
     pairs = [(source, source ^ 1) for source in range(groups)]
     dma = pltpu.SemaphoreType.DMA
@@ -336,15 +331,14 @@
         pack_kernel,
         [bf16(groups, kept_max, LANES), bf16(head // 2, width), token],
         [HBM] * 6,
-        [VMEM, HBM, VMEM],
+        [VMEM] * 3,
         [
             pltpu.SMEM((2, images), jnp.int32),
             pltpu.SMEM((1, images), jnp.int32),
             pltpu.SMEM((1, images), jnp.int32),
             pltpu.VMEM((images, kept_max), jnp.int32),
             pltpu.VMEM((images, patch_max, patch_width), jnp.bfloat16),
-            pltpu.VMEM((head // 2, width), jnp.bfloat16),
-            dma((6,)),
+            dma((5,)),
             dma((parts,)),
         ],
         60,

time: 59.1 us -> 58.4 us (0.988)
  Pallas kernels: 27.5 us -> 26.8 us
    pallas_call x1, Pallas kernels: 3.8 us -> 3.11 us  [shards(): call(pack_kernel, [bf16(groups, kept_max, LANES), bf16(head // 2, width),...]
  transfers between devices with their start and end apart: 5 -> 5, of which waited for: 2 -> 2; matrix products, arithmetic and copies ran while one was open for 0% -> 0% of each run, Pallas kernels for 35% -> 36%
where the time goes in v5:
time: 58.4 us; the launch traced here: 57.5 us
  Pallas kernels  26.8 us (46%)
  starting transfers between devices  16 us (27%)
  waiting for transfers between devices  8.72 us (15%)
  local copies, waits for them, and re-layouts  5.51 us (9%)
    pallas_call x1, Pallas kernels, shards(): call(attend_kernel, [bf16(seq_len, head), bf16(tiles - 2, LANES, TILE), t...  11 us
    all_to_all x1, starting transfers between devices, shards(): lax.all_to_all(packed, 'dp', split_axis=0, concat_axis=0, tiled=True)  9.74 us
    all_to_all x1, waiting for transfers between devices, shards(): lax.all_to_all(packed, 'dp', split_axis=0, concat_axis=0, tiled=True)  7.44 us
    unnamed x14, local copies, waits for them, and re-layouts  5.42 us
    pallas_call x1, Pallas kernels, shards(): call(weight_kernel, [bf16(STORE, TILE), bf16(1, LANES, TILE)], [HBM] + [V...  4.69 us
    pallas_call x1, Pallas kernels, shards(): call(embed_kernel, [jax.ShapeDtypeStruct((seq_len, width), jnp.float32),...  3.5 us
    pallas_call x1, Pallas kernels, shards(): call(section_kernel, bf16(1, seq_len, width), [VMEM] * 8, HBM, [pltpu.VME...  3.19 us
    pallas_call x1, Pallas kernels, shards(): call(pack_kernel, [bf16(groups, kept_max, LANES), bf16(head // 2, width),...  3.11 us
  transfers between devices with their start and end apart: 5, of which 2 were waited for; matrix products, arithmetic and copies ran while one was open for 0% of the time, Pallas kernels for 36%

profile of v5, /device:TPU:1, one launch (start us, length us, event | category | flops | bytes accessed | tf_op | source)
XLA Modules:
  0.0 57.5 jit_solution(2678733454106882399)
XLA Ops:
  0.0 3.1 %shard_map.118 = (bf16[32,32,640]{2,1,0:T(8,128)(2,1)}, bf16[64,6144]{1,0:T(8,128)(2,1)}, f32[8,128]{1,0:T(8,128)}) custom-call(s32[2,16]{1,0:T(2,128)} %bitcast.13, s32[1,16]{1,0:T(1,128)} %count_hbm.1, s32[1,16]{1,0:T(1,128)} %dest_hbm.1, s32[16,32]{1,0:T(8,128)} %bitcast.12, bf16[16,64,588]{2,1,0:T(8,128)(2,1)} %bitcast.11, bf16[128,6144]{1,0:T(8,128)(2,1)} %bitcast.10), custom_call_target="tpu_custom_call" | custom-call | flops 41943040 | bytes 1048576 | tf_op jit(solution)/shard_map/pallas_call | solution.py:330
  3.1 0.0 slice-start
  3.1 0.0 copy-start.5
  3.1 0.0 copy-start.6
  3.2 9.7 %all-to-all-start = ((bf16[32,32,640]{2,1,0:T(8,128)(2,1)}), bf16[32,32,640]{2,1,0:T(8,128)(2,1)S(1)}, u32[]{:S(2)}, u32[]{:S(2)}) async-start(bf16[32,32,640]{2,1,0:T(8,128)(2,1)} %get-tuple-element.19), calls=%async_computation | async-start | bytes 2621440 | tf_op jit(solution)/shard_map/all_to_all | solution.py:347
  12.9 1.3 %collective-permute-start.1 = (bf16[64,6144]{1,0:T(8,128)(2,1)}, bf16[64,6144]{1,0:T(8,128)(2,1)S(1)}, u32[]{:S(2)}, u32[]{:S(2)}) collective-permute-start(bf16[64,6144]{1,0:T(8,128)(2,1)} %get-tuple-element.25), channel_id=1, source_target_pairs={{0,1},{1,2},{2,3},{3,0},{4,5},{5,6},{6,7},{7,4},{8,9},{9,10},{10,1... | collective-permute-start | bytes 2359304 | tf_op jit(solution)/shard_map/ppermute | solution.py:349
  14.2 0.1 pad.3.clone
  14.3 0.2 maximum_maximum_fusion.tail_ref
  14.5 0.0 copy-start
  14.5 3.1 %copy-done = bf16[588,6144]{1,0:T(8,128)(2,1)S(1)} copy-done((bf16[588,6144]{1,0:T(8,128)(2,1)S(1)}, bf16[588,6144]{1,0:T(8,128)(2,1)}, u32[]{:S(2)}) %copy-start) | copy-done | bytes 7225368
  17.5 2.3 %copy-done.1 = bf16[1,6144,384]{2,1,0:T(8,128)(2,1)S(1)} copy-done((bf16[1,6144,384]{2,1,0:T(8,128)(2,1)S(1)}, bf16[1,6144,384]{2,1,0:T(8,128)(2,1)}, u32[]{:S(2)}) %copy-start.1) | copy-done | bytes 4718616
  19.9 4.7 %shard_map.119 = (bf16[20480,1024]{1,0:T(8,128)(2,1)}, bf16[1,640,1024]{2,1,0:T(8,128)(2,1)S(1)}) custom-call(f32[8,128]{1,0:T(8,128)S(1)} %copy-done.3, bf16[588,6144]{1,0:T(8,128)(2,1)S(1)} %copy-done, bf16[64,6144]{1,0:T(8,128)(2,1)S(1)} %maximum_maximum_fusion.tail_ref, bf16[6144,384]{1,0:T(8,128)(2,1)S(1)} %bitcast.8), custom_call_target="tpu_custom_call" | custom-call | flops 1048576 | bytes 1048576 | tf_op jit(solution)/shard_map/pallas_call | solution.py:359
  24.6 7.4 %all-to-all-done.recv_ref = bf16[32,32,640]{2,1,0:T(8,128)(2,1)S(1)} async-done(((bf16[32,32,640]{2,1,0:T(8,128)(2,1)}), bf16[32,32,640]{2,1,0:T(8,128)(2,1)S(1)}, u32[]{:S(2)}, u32[]{:S(2)}) %all-to-all-start) | async-done | bytes 1310752 | tf_op jit(solution)/shard_map/all_to_all | solution.py:347
  32.0 1.4 %shard_map.120 = (bf16[512,640]{1,0:T(8,128)(2,1)S(1)}, bf16[1,640,1024]{2,1,0:T(8,128)(2,1)S(1)}) custom-call(bf16[20480,1024]{1,0:T(8,128)(2,1)} %get-tuple-element.18.weights_hbm, bf16[32,32,640]{2,1,0:T(8,128)(2,1)S(1)} %all-to-all-done.recv_ref), custom_call_target="tpu_custom_call" | custom-call | flops 671088640 | bytes 1048576 | tf_op jit(solution)/shard_map/pallas_call | solution.py:368
  33.4 1.5 %collective-permute-start = (bf16[512,640]{1,0:T(8,128)(2,1)S(1)}, bf16[512,640]{1,0:T(8,128)(2,1)S(1)}, u32[]{:S(2)}, u32[]{:S(2)}) collective-permute-start(bf16[512,640]{1,0:T(8,128)(2,1)S(1)} %get-tuple-element.20.x_ref), channel_id=1, source_target_pairs={{0,1},{1,2},{2,3},{3,0},{4,5},{5,6},{6,7},{7,4},{8,9},{9,10},{10,1... | collective-permute-start | bytes 1966088 | tf_op jit(solution)/shard_map/ppermute | solution.py:377
  34.8 11.0 %shard_map.121 = (bf16[512,128]{1,0:T(8,128)(2,1)S(1)}, bf16[4,640,1024]{2,1,0:T(8,128)(2,1)S(1)}, f32[8,128]{1,0:T(8,128)S(1)}) custom-call(bf16[512,640]{1,0:T(8,128)(2,1)S(1)} %get-tuple-element.20.x_ref, bf16[1,6144]{1,0:T(2,128)(2,1)S(1)} %copy-done.2, f32[2,128]{1,0:T(2,128)S(1)} %bitcast.9, bf16[1,640,1024]{2,1,0:T(8,128)(2,1)S(1)} %get-tuple-element.21.tile_ref, ...), custom_call_target="tpu_custom_call" | custom-call | flops 6442450944 | bytes 1048576 | tf_op jit(solution)/shard_map/pallas_call | solution.py:378
  45.8 0.0 collective-permute-done.1.half_hbm
  45.8 2.3 %collective-permute-start.3 = (bf16[64,6144]{1,0:T(8,128)(2,1)S(1)}, bf16[64,6144]{1,0:T(8,128)(2,1)S(1)}, u32[]{:S(2)}, u32[]{:S(2)}) collective-permute-start(bf16[64,6144]{1,0:T(8,128)(2,1)S(1)} %shard_map.122.half_hbm), channel_id=1, source_target_pairs={{0,4},{4,0},{8,12},{12,8},{16,20},{20,16},{24,28},{28,24},{32,36},... | collective-permute-start | bytes 2359304 | tf_op jit(solution)/shard_map/ppermute | solution.py:396
  48.1 1.2 %collective-permute-start.2 = (bf16[512,128]{1,0:T(8,128)(2,1)S(1)}, bf16[512,128]{1,0:T(8,128)(2,1)S(1)}, u32[]{:S(2)}, u32[]{:S(2)}) collective-permute-start(bf16[512,128]{1,0:T(8,128)(2,1)S(1)} %get-tuple-element.27), channel_id=1, source_target_pairs={{0,1},{1,2},{2,3},{3,0},{4,5},{5,6},{6,7},{7,4},{8,9},{9,10},{10,1... | collective-permute-start | bytes 393224 | tf_op jit(solution)/shard_map/ppermute | solution.py:392
  49.3 0.0 collective-permute-done.x_ref
  49.3 3.5 %shard_map.123 = (f32[512,6144]{1,0:T(8,128)S(1)}, bf16[64,6144]{1,0:T(8,128)(2,1)S(1)}) custom-call(bf16[512,640]{1,0:T(8,128)(2,1)S(1)} %collective-permute-done.x_ref, bf16[1,640,1024]{2,1,0:T(8,128)(2,1)S(1)} %get-tuple-element.21.tile_ref, bf16[1,640,1024]{2,1,0:T(8,128)(2,1)S(1)} %get-tuple-element.22.early_ref, ...), custom_call_target="tpu_custom_call" | custom-call | flops 4026531840 | bytes 1048576 | tf_op jit(solution)/shard_map/pallas_call | solution.py:398
  52.9 1.3 %collective-permute-done.2.attended_ref = bf16[512,128]{1,0:T(8,128)(2,1)S(1)} collective-permute-done((bf16[512,128]{1,0:T(8,128)(2,1)S(1)}, bf16[512,128]{1,0:T(8,128)(2,1)S(1)}, u32[]{:S(2)}, u32[]{:S(2)}) %collective-permute-start.2) | collective-permute-done | bytes 131104 | tf_op jit(solution)/shard_map/ppermute | solution.py:392
  54.1 0.0 collective-permute-done.3.other_ref
  54.1 3.2 %shard_map.124 = bf16[1,512,6144]{2,1,0:T(8,128)(2,1)} custom-call(f32[512,6144]{1,0:T(8,128)S(1)} %get-tuple-element.26.part_ref, bf16[512,640]{1,0:T(8,128)(2,1)S(1)} %collective-permute-done.x_ref, bf16[512,128]{1,0:T(8,128)(2,1)S(1)} %collective-permute-done.2.attended_ref, bf16[1,640,1024]{2,1,0:T(8,128)(2,1)S(1)} %get-tuple-element.21.tile_ref, ...), custom_call_target="tpu_custom_call" | custom-call | flops 805306368 | bytes 1048576 | tf_op jit(solution)/shard_map/pallas_call | solution.py:407
  (12 shorter events, 0.0 us)
Async XLA Ops:
  3.1 11.2 %slice-start = ((bf16[588,6144]{1,0:T(8,128)(2,1)}), bf16[12,6144]{1,0:T(8,128)(2,1)S(1)}, s32[]{:S(2)}) async-start(bf16[588,6144]{1,0:T(8,128)(2,1)} %embed_ref.1), calls=%async_computation.1 | async-start | bytes 393216 | tf_op jit(solution)/shard_map/slice | solution.py:352
  3.1 11.2 %copy-start.5 = (bf16[8,6144]{1,0:T(8,128)(2,1)S(1)}, bf16[8,6144]{1,0:T(8,128)(2,1)}, u32[]{:S(2)}) copy-start(bf16[8,6144]{1,0:T(8,128)(2,1)} %param.19) | copy-start | bytes 294916
  3.1 11.1 %copy-start.6 = (bf16[8,6144]{1,0:T(8,128)(2,1)S(1)}, bf16[8,6144]{1,0:T(8,128)(2,1)}, u32[]{:S(2)}) copy-start(bf16[8,6144]{1,0:T(8,128)(2,1)} %param.18) | copy-start | bytes 294916
  3.2 11.3 %copy-start.3 = (f32[8,128]{1,0:T(8,128)S(1)}, f32[8,128]{1,0:T(8,128)}, u32[]{:S(2)}) copy-start(f32[8,128]{1,0:T(8,128)} %get-tuple-element.17.token_hbm) | copy-start | bytes 12292
  3.2 28.8 %all-to-all-start = ((bf16[32,32,640]{2,1,0:T(8,128)(2,1)}), bf16[32,32,640]{2,1,0:T(8,128)(2,1)S(1)}, u32[]{:S(2)}, u32[]{:S(2)}) async-start(bf16[32,32,640]{2,1,0:T(8,128)(2,1)} %get-tuple-element.19), calls=%async_computation | async-start | bytes 2621440 | tf_op jit(solution)/shard_map/all_to_all | solution.py:347
  12.9 32.9 %collective-permute-start.1 = (bf16[64,6144]{1,0:T(8,128)(2,1)}, bf16[64,6144]{1,0:T(8,128)(2,1)S(1)}, u32[]{:S(2)}, u32[]{:S(2)}) collective-permute-start(bf16[64,6144]{1,0:T(8,128)(2,1)} %get-tuple-element.25), channel_id=1, source_target_pairs={{0,1},{1,2},{2,3},{3,0},{4,5},{5,6},{6,7},{7,4},{8,9},{9,10},{10,1... | collective-permute-start | bytes 2359304 | tf_op jit(solution)/shard_map/ppermute | solution.py:349
  14.5 3.1 %copy-start = (bf16[588,6144]{1,0:T(8,128)(2,1)S(1)}, bf16[588,6144]{1,0:T(8,128)(2,1)}, u32[]{:S(2)}) copy-start(bf16[588,6144]{1,0:T(8,128)(2,1)} %embed_ref.1) | copy-start | bytes 21676036
  17.5 2.3 %copy-start.1 = (bf16[1,6144,384]{2,1,0:T(8,128)(2,1)S(1)}, bf16[1,6144,384]{2,1,0:T(8,128)(2,1)}, u32[]{:S(2)}) copy-start(bf16[1,6144,384]{2,1,0:T(8,128)(2,1)} %param.21) | copy-start | bytes 14155780
  32.0 2.8 %copy-start.2 = (bf16[1,6144]{1,0:T(2,128)(2,1)S(1)}, bf16[1,6144]{1,0:T(2,128)(2,1)}, u32[]{:S(2)}) copy-start(bf16[1,6144]{1,0:T(2,128)(2,1)} %gain_ref.1) | copy-start | bytes 36868
  32.0 2.8 %copy-start.4 = (f32[1,2,128]{2,1,0:T(2,128)S(1)}, f32[1,2,128]{2,1,0:T(2,128)}, u32[]{:S(2)}) copy-start(f32[1,2,128]{2,1,0:T(2,128)} %param.22) | copy-start | bytes 3076
  33.4 16.0 %collective-permute-start = (bf16[512,640]{1,0:T(8,128)(2,1)S(1)}, bf16[512,640]{1,0:T(8,128)(2,1)S(1)}, u32[]{:S(2)}, u32[]{:S(2)}) collective-permute-start(bf16[512,640]{1,0:T(8,128)(2,1)S(1)} %get-tuple-element.20.x_ref), channel_id=1, source_target_pairs={{0,1},{1,2},{2,3},{3,0},{4,5},{5,6},{6,7},{7,4},{8,9},{9,10},{10,1... | collective-permute-start | bytes 1966088 | tf_op jit(solution)/shard_map/ppermute | solution.py:377
  45.8 8.3 %collective-permute-start.3 = (bf16[64,6144]{1,0:T(8,128)(2,1)S(1)}, bf16[64,6144]{1,0:T(8,128)(2,1)S(1)}, u32[]{:S(2)}, u32[]{:S(2)}) collective-permute-start(bf16[64,6144]{1,0:T(8,128)(2,1)S(1)} %shard_map.122.half_hbm), channel_id=1, source_target_pairs={{0,4},{4,0},{8,12},{12,8},{16,20},{20,16},{24,28},{28,24},{32,36},... | collective-permute-start | bytes 2359304 | tf_op jit(solution)/shard_map/ppermute | solution.py:396
  48.1 6.0 %collective-permute-start.2 = (bf16[512,128]{1,0:T(8,128)(2,1)S(1)}, bf16[512,128]{1,0:T(8,128)(2,1)S(1)}, u32[]{:S(2)}, u32[]{:S(2)}) collective-permute-start(bf16[512,128]{1,0:T(8,128)(2,1)S(1)} %get-tuple-element.27), channel_id=1, source_target_pairs={{0,1},{1,2},{2,3},{3,0},{4,5},{5,6},{6,7},{7,4},{8,9},{9,10},{10,1... | collective-permute-start | bytes 393224 | tf_op jit(solution)/shard_map/ppermute | solution.py:392

commit v6 on v5

--- a/solution.py
+++ b/solution.py
@@ -245,31 +245,40 @@
         out_ref[here, :] = attended.astype(jnp.bfloat16)
 
 
-def embed_kernel(x_ref, tile_ref, early_ref, late_ref, half_hbm, out_ref, half_ref, sem):
-    copy = pltpu.make_async_copy(half_hbm, half_ref, sem.at[0])
+def join_kernel(tile_ref, early_ref, late_ref, half_hbm, out_ref, token_ref, half, sem):
+    copy = pltpu.make_async_copy(half_hbm, half, sem.at[0])
     copy.start()
+    token_ref[...] = jnp.zeros_like(token_ref)
+    last = LANES - TAIL
+    share = half.shape[0]
+    core = lax.axis_index("dp") % 2
+    for t in range(2 + late_ref.shape[0]):
+        tile = (tile_ref[0, TAIL:], early_ref[0, TAIL:])[t] if t < 2 else late_ref[t - 2, TAIL:]
+        out_ref[:last, t * TILE : (t + 1) * TILE] = tile
+    out_ref[pl.ds(pl.multiple_of(last + (1 - core) * share, share), share), :] = jnp.zeros_like(half)
+    copy.wait()
+    out_ref[pl.ds(pl.multiple_of(last + core * share, share), share), :] = half[...]
+
+
+def embed_kernel(token_hbm, x_ref, tile_ref, early_ref, late_ref, out_ref):
     for t in range(2 + late_ref.shape[0]):
         span = slice(t * TILE, (t + 1) * TILE)
         tile = (tile_ref[0, :TAIL], early_ref[0, :TAIL])[t] if t < 2 else late_ref[t - 2, :TAIL]
         out_ref[:, span] = dot(x_ref[:, :TAIL], tile)
-    copy.wait()
 
 
 def section_kernel(
-    part_ref, x_ref, attended_ref, tile_ref, early_ref, late_ref, mine_ref, other_ref, out_hbm, weight, out, sems
+    part_ref, x_ref, attended_ref, joined_ref, other_ref, out_hbm, weight_ref, out, sems
 ):
-    half = mine_ref.shape[0]
-    last = x_ref.shape[1] - TAIL
+    share = other_ref.shape[0]
     core = lax.axis_index("dp") % 2
-    weight[pl.ds(pl.multiple_of(last + core * half, half), half), :] = mine_ref[...]
-    weight[pl.ds(pl.multiple_of(last + (1 - core) * half, half), half), :] = other_ref[...]
+    first = weight_ref.shape[0] - (1 + core) * share
+    weight_ref[pl.ds(pl.multiple_of(first, share), share), :] = other_ref[...]
     both = jnp.concatenate([x_ref[:, TAIL:], attended_ref[...]], axis=1)
     results = []
     for t in range(out.shape[1] // TILE):
         span = slice(t * TILE, (t + 1) * TILE)
-        tile = (tile_ref[0, TAIL:], early_ref[0, TAIL:])[t] if t < 2 else late_ref[t - 2, TAIL:]
-        weight[:last, span] = tile
-        out[:, span] = (part_ref[:, span] + dot(both, weight[:, span])).astype(jnp.bfloat16)
+        out[:, span] = (part_ref[:, span] + dot(both, weight_ref[:, span])).astype(jnp.bfloat16)
         columns = pl.ds(t * TILE, TILE)
         result = pltpu.make_async_copy(out.at[:, columns], out_hbm.at[0, :, columns], sems.at[t])
         result.start()
@@ -395,28 +404,35 @@
     )
     other = lax.ppermute(half, "dp", pairs)
 
-    part, half = call(
+    joined, after_join = call(
+        join_kernel,
+        [bf16(LANES - TAIL + head, width), token],
+        [VMEM] * 3 + [HBM],
+        [VMEM] * 2,
+        [pltpu.VMEM((head // 2, width), jnp.bfloat16), dma((1,))],
+        12,
+        MIB,
+    )(tile, early, late, half)
+    part = call(
         embed_kernel,
-        [jax.ShapeDtypeStruct((seq_len, width), jnp.float32), bf16(head // 2, width)],
-        [VMEM] * 4 + [HBM],
-        [VMEM] * 2,
-        [dma((1,))],
+        jax.ShapeDtypeStruct((seq_len, width), jnp.float32),
+        [HBM] + [VMEM] * 4,
+        VMEM,
+        [],
         16,
         2 * seq_len * width * LANES,
-    )(next_x, tile, early, late, half)
-    return call(
+    )(after_join, next_x, tile, early, late)
+    out, _ = call(
         section_kernel,
-        bf16(1, seq_len, width),
-        [VMEM] * 8,
-        HBM,
-        [
-            pltpu.VMEM((LANES - TAIL + head, width), jnp.bfloat16),
-            pltpu.VMEM((seq_len, width), jnp.bfloat16),
-            dma((tiles,)),
-        ],
+        [bf16(1, seq_len, width), bf16(LANES - TAIL + head, width)],
+        [VMEM] * 5,
+        [HBM, VMEM],
+        [pltpu.VMEM((seq_len, width), jnp.bfloat16), dma((tiles,))],
         20,
         2 * seq_len * width * head,
-    )(part, next_x, next_attended, tile, early, late, half, other)
+        {3: 1},
+    )(part, next_x, next_attended, joined, other)
+    return out
 
 
 def solution(mesh):

time: 58.4 us -> 58.4 us (level)
  waiting for transfers between devices: 8.72 us -> 7.59 us
  Pallas kernels: 26.8 us -> 27.9 us
    ppermute x1, waiting for transfers between devices: 1.28 us -> 0.14 us  [shards(): next_attended = lax.ppermute(attended, 'segment', onward)]
    pallas_call x2 -> x3, Pallas kernels: 6.69 us -> 7.81 us  [the longest x1 3.44 us: shards(): call(embed_kernel, jax.ShapeDtypeStruct((seq_len, width), jnp.float32), [...]
  transfers between devices with their start and end apart: 5 -> 5, of which waited for: 2 -> 2; matrix products, arithmetic and copies ran while one was open for 0% -> 0% of each run, Pallas kernels for 36% -> 38%
where the time goes in v6:
time: 58.4 us; the launch traced here: 57.5 us
  Pallas kernels  27.9 us (48%)
  starting transfers between devices  16 us (27%)
  waiting for transfers between devices  7.59 us (13%)
  local copies, waits for them, and re-layouts  5.51 us (9%)
    pallas_call x1, Pallas kernels, shards(): call(attend_kernel, [bf16(seq_len, head), bf16(tiles - 2, LANES, TILE), t...  11 us
    all_to_all x1, starting transfers between devices, shards(): lax.all_to_all(packed, 'dp', split_axis=0, concat_axis=0, tiled=True)  9.74 us
    all_to_all x1, waiting for transfers between devices, shards(): lax.all_to_all(packed, 'dp', split_axis=0, concat_axis=0, tiled=True)  7.44 us
    unnamed x14, local copies, waits for them, and re-layouts  5.42 us
    pallas_call x1, Pallas kernels, shards(): call(weight_kernel, [bf16(STORE, TILE), bf16(1, LANES, TILE)], [HBM] + [V...  4.69 us
    pallas_call x1, Pallas kernels, shards(): call(embed_kernel, jax.ShapeDtypeStruct((seq_len, width), jnp.float32), [...  3.44 us
    pallas_call x1, Pallas kernels, shards(): call(section_kernel, [bf16(1, seq_len, width), bf16(LANES - TAIL + head,...  3.18 us
    pallas_call x1, Pallas kernels, shards(): call(pack_kernel, [bf16(groups, kept_max, LANES), bf16(head // 2, width),...  3.11 us
  transfers between devices with their start and end apart: 5, of which 2 were waited for; matrix products, arithmetic and copies ran while one was open for 0% of the time, Pallas kernels for 38%

profile of v6, /device:TPU:1, one launch (start us, length us, event | category | flops | bytes accessed | tf_op | source)
XLA Modules:
  0.0 57.5 jit_solution(17520897790201840687)
XLA Ops:
  0.0 3.1 %shard_map.118 = (bf16[32,32,640]{2,1,0:T(8,128)(2,1)}, bf16[64,6144]{1,0:T(8,128)(2,1)}, f32[8,128]{1,0:T(8,128)}) custom-call(s32[2,16]{1,0:T(2,128)} %bitcast.13, s32[1,16]{1,0:T(1,128)} %count_hbm.1, s32[1,16]{1,0:T(1,128)} %dest_hbm.1, s32[16,32]{1,0:T(8,128)} %bitcast.12, bf16[16,64,588]{2,1,0:T(8,128)(2,1)} %bitcast.11, bf16[128,6144]{1,0:T(8,128)(2,1)} %bitcast.10), custom_call_target="tpu_custom_call" | custom-call | flops 41943040 | bytes 1048576 | tf_op jit(solution)/shard_map/pallas_call | solution.py:339
  3.1 0.0 slice-start
  3.1 0.0 copy-start.5
  3.1 0.0 copy-start.6
  3.2 9.7 %all-to-all-start = ((bf16[32,32,640]{2,1,0:T(8,128)(2,1)}), bf16[32,32,640]{2,1,0:T(8,128)(2,1)S(1)}, u32[]{:S(2)}, u32[]{:S(2)}) async-start(bf16[32,32,640]{2,1,0:T(8,128)(2,1)} %get-tuple-element.21), calls=%async_computation | async-start | bytes 2621440 | tf_op jit(solution)/shard_map/all_to_all | solution.py:356
  12.9 1.3 %collective-permute-start = (bf16[64,6144]{1,0:T(8,128)(2,1)}, bf16[64,6144]{1,0:T(8,128)(2,1)}, u32[]{:S(2)}, u32[]{:S(2)}) collective-permute-start(bf16[64,6144]{1,0:T(8,128)(2,1)} %get-tuple-element.26), channel_id=1, source_target_pairs={{0,1},{1,2},{2,3},{3,0},{4,5},{5,6},{6,7},{7,4},{8,9},{9,10},{10,1... | collective-permute-start | bytes 2359304 | tf_op jit(solution)/shard_map/ppermute | solution.py:358
  14.2 0.1 pad.3.clone
  14.3 0.2 maximum_maximum_fusion.tail_ref
  14.5 0.0 copy-start
  14.5 3.1 %copy-done = bf16[588,6144]{1,0:T(8,128)(2,1)S(1)} copy-done((bf16[588,6144]{1,0:T(8,128)(2,1)S(1)}, bf16[588,6144]{1,0:T(8,128)(2,1)}, u32[]{:S(2)}) %copy-start) | copy-done | bytes 7225368
  17.5 2.3 %copy-done.1 = bf16[1,6144,384]{2,1,0:T(8,128)(2,1)S(1)} copy-done((bf16[1,6144,384]{2,1,0:T(8,128)(2,1)S(1)}, bf16[1,6144,384]{2,1,0:T(8,128)(2,1)}, u32[]{:S(2)}) %copy-start.1) | copy-done | bytes 4718616
  19.9 4.7 %shard_map.119 = (bf16[20480,1024]{1,0:T(8,128)(2,1)}, bf16[1,640,1024]{2,1,0:T(8,128)(2,1)S(1)}) custom-call(f32[8,128]{1,0:T(8,128)S(1)} %copy-done.3, bf16[588,6144]{1,0:T(8,128)(2,1)S(1)} %copy-done, bf16[64,6144]{1,0:T(8,128)(2,1)S(1)} %maximum_maximum_fusion.tail_ref, bf16[6144,384]{1,0:T(8,128)(2,1)S(1)} %bitcast.8), custom_call_target="tpu_custom_call" | custom-call | flops 1048576 | bytes 1048576 | tf_op jit(solution)/shard_map/pallas_call | solution.py:368
  24.6 7.4 %all-to-all-done.recv_ref = bf16[32,32,640]{2,1,0:T(8,128)(2,1)S(1)} async-done(((bf16[32,32,640]{2,1,0:T(8,128)(2,1)}), bf16[32,32,640]{2,1,0:T(8,128)(2,1)S(1)}, u32[]{:S(2)}, u32[]{:S(2)}) %all-to-all-start) | async-done | bytes 1310752 | tf_op jit(solution)/shard_map/all_to_all | solution.py:356
  32.0 1.4 %shard_map.120 = (bf16[512,640]{1,0:T(8,128)(2,1)S(1)}, bf16[1,640,1024]{2,1,0:T(8,128)(2,1)S(1)}) custom-call(bf16[20480,1024]{1,0:T(8,128)(2,1)} %get-tuple-element.20.weights_hbm, bf16[32,32,640]{2,1,0:T(8,128)(2,1)S(1)} %all-to-all-done.recv_ref), custom_call_target="tpu_custom_call" | custom-call | flops 671088640 | bytes 1048576 | tf_op jit(solution)/shard_map/pallas_call | solution.py:377
  33.4 1.5 %collective-permute-start.1 = (bf16[512,640]{1,0:T(8,128)(2,1)S(1)}, bf16[512,640]{1,0:T(8,128)(2,1)S(1)}, u32[]{:S(2)}, u32[]{:S(2)}) collective-permute-start(bf16[512,640]{1,0:T(8,128)(2,1)S(1)} %get-tuple-element.23.x_ref), channel_id=1, source_target_pairs={{0,1},{1,2},{2,3},{3,0},{4,5},{5,6},{6,7},{7,4},{8,9},{9,10},{10,1... | collective-permute-start | bytes 1966088 | tf_op jit(solution)/shard_map/ppermute | solution.py:386
  34.8 11.0 %shard_map.121 = (bf16[512,128]{1,0:T(8,128)(2,1)S(1)}, bf16[4,640,1024]{2,1,0:T(8,128)(2,1)S(1)}, f32[8,128]{1,0:T(8,128)S(1)}) custom-call(bf16[512,640]{1,0:T(8,128)(2,1)S(1)} %get-tuple-element.23.x_ref, bf16[1,6144]{1,0:T(2,128)(2,1)S(1)} %copy-done.2, f32[2,128]{1,0:T(2,128)S(1)} %bitcast.9, bf16[1,640,1024]{2,1,0:T(8,128)(2,1)S(1)} %get-tuple-element.19.tile_ref, ...), custom_call_target="tpu_custom_call" | custom-call | flops 6442450944 | bytes 1048576 | tf_op jit(solution)/shard_map/pallas_call | solution.py:387
  45.8 0.0 collective-permute-done.half_hbm
  45.8 2.3 %collective-permute-start.3 = (bf16[64,6144]{1,0:T(8,128)(2,1)}, bf16[64,6144]{1,0:T(8,128)(2,1)S(1)}, u32[]{:S(2)}, u32[]{:S(2)}) collective-permute-start(bf16[64,6144]{1,0:T(8,128)(2,1)} %shard_map.122.half_hbm), channel_id=1, source_target_pairs={{0,4},{4,0},{8,12},{12,8},{16,20},{20,16},{24,28},{28,24},{32,36},... | collective-permute-start | bytes 2359304 | tf_op jit(solution)/shard_map/ppermute | solution.py:405
  48.1 1.2 %collective-permute-start.2 = (bf16[512,128]{1,0:T(8,128)(2,1)S(1)}, bf16[512,128]{1,0:T(8,128)(2,1)S(1)}, u32[]{:S(2)}, u32[]{:S(2)}) collective-permute-start(bf16[512,128]{1,0:T(8,128)(2,1)S(1)} %get-tuple-element.28), channel_id=1, source_target_pairs={{0,1},{1,2},{2,3},{3,0},{4,5},{5,6},{6,7},{7,4},{8,9},{9,10},{10,1... | collective-permute-start | bytes 393224 | tf_op jit(solution)/shard_map/ppermute | solution.py:401
  49.3 1.2 %shard_map.123 = (bf16[256,6144]{1,0:T(8,128)(2,1)S(1)}, f32[8,128]{1,0:T(8,128)S(1)}) custom-call(bf16[1,640,1024]{2,1,0:T(8,128)(2,1)S(1)} %get-tuple-element.19.tile_ref, bf16[1,640,1024]{2,1,0:T(8,128)(2,1)S(1)} %get-tuple-element.22.early_ref, bf16[4,640,1024]{2,1,0:T(8,128)(2,1)S(1)} %get-tuple-element.24.late_ref, bf16[64,6144]{1,0:T(8,128)(2,1)} %shard_map.122.half_hbm), custom_call_target="tpu_custom_call" | custom-call | flops 1048576 | bytes 1048576 | tf_op jit(solution)/shard_map/pallas_call | solution.py:407
  50.5 3.4 %shard_map.124.part_ref = f32[512,6144]{1,0:T(8,128)S(1)} custom-call(f32[8,128]{1,0:T(8,128)S(1)} %get-tuple-element.27.token_hbm, bf16[512,640]{1,0:T(8,128)(2,1)S(1)} %collective-permute-done.1.x_ref, bf16[1,640,1024]{2,1,0:T(8,128)(2,1)S(1)} %get-tuple-element.19.tile_ref, bf16[1,640,1024]{2,1,0:T(8,128)(2,1)S(1)} %get-tuple-element.22.early_ref, ...), custom_call_target="tpu_custom_call" | custom-call | flops 4026531840 | bytes 1048576 | tf_op jit(solution)/shard_map/pallas_call | solution.py:416
  54.0 0.1 collective-permute-done.2.attended_ref
  54.1 0.0 collective-permute-done.3.other_ref
  54.1 3.2 %shard_map.125 = (bf16[1,512,6144]{2,1,0:T(8,128)(2,1)}, bf16[256,6144]{1,0:T(8,128)(2,1)S(1)}) custom-call(f32[512,6144]{1,0:T(8,128)S(1)} %shard_map.124.part_ref, bf16[512,640]{1,0:T(8,128)(2,1)S(1)} %collective-permute-done.1.x_ref, bf16[512,128]{1,0:T(8,128)(2,1)S(1)} %collective-permute-done.2.attended_ref, ...), custom_call_target="tpu_custom_call", output_to_operand_aliasing={{1}: (3, {})} | custom-call | flops 805306368 | bytes 1048576 | tf_op jit(solution)/shard_map/pallas_call | solution.py:425
  (13 shorter events, 0.0 us)
Async XLA Ops:
  3.1 11.2 %slice-start = ((bf16[588,6144]{1,0:T(8,128)(2,1)}), bf16[12,6144]{1,0:T(8,128)(2,1)S(1)}, s32[]{:S(2)}) async-start(bf16[588,6144]{1,0:T(8,128)(2,1)} %embed_ref.1), calls=%async_computation.1 | async-start | bytes 393216 | tf_op jit(solution)/shard_map/slice | solution.py:361
  3.1 11.2 %copy-start.5 = (bf16[8,6144]{1,0:T(8,128)(2,1)S(1)}, bf16[8,6144]{1,0:T(8,128)(2,1)}, u32[]{:S(2)}) copy-start(bf16[8,6144]{1,0:T(8,128)(2,1)} %param.19) | copy-start | bytes 294916
  3.1 11.1 %copy-start.6 = (bf16[8,6144]{1,0:T(8,128)(2,1)S(1)}, bf16[8,6144]{1,0:T(8,128)(2,1)}, u32[]{:S(2)}) copy-start(bf16[8,6144]{1,0:T(8,128)(2,1)} %param.18) | copy-start | bytes 294916
  3.2 11.3 %copy-start.3 = (f32[8,128]{1,0:T(8,128)S(1)}, f32[8,128]{1,0:T(8,128)}, u32[]{:S(2)}) copy-start(f32[8,128]{1,0:T(8,128)} %get-tuple-element.18.token_hbm) | copy-start | bytes 12292
  3.2 28.8 %all-to-all-start = ((bf16[32,32,640]{2,1,0:T(8,128)(2,1)}), bf16[32,32,640]{2,1,0:T(8,128)(2,1)S(1)}, u32[]{:S(2)}, u32[]{:S(2)}) async-start(bf16[32,32,640]{2,1,0:T(8,128)(2,1)} %get-tuple-element.21), calls=%async_computation | async-start | bytes 2621440 | tf_op jit(solution)/shard_map/all_to_all | solution.py:356
  12.9 32.9 %collective-permute-start = (bf16[64,6144]{1,0:T(8,128)(2,1)}, bf16[64,6144]{1,0:T(8,128)(2,1)}, u32[]{:S(2)}, u32[]{:S(2)}) collective-permute-start(bf16[64,6144]{1,0:T(8,128)(2,1)} %get-tuple-element.26), channel_id=1, source_target_pairs={{0,1},{1,2},{2,3},{3,0},{4,5},{5,6},{6,7},{7,4},{8,9},{9,10},{10,1... | collective-permute-start | bytes 2359304 | tf_op jit(solution)/shard_map/ppermute | solution.py:358
  14.5 3.1 %copy-start = (bf16[588,6144]{1,0:T(8,128)(2,1)S(1)}, bf16[588,6144]{1,0:T(8,128)(2,1)}, u32[]{:S(2)}) copy-start(bf16[588,6144]{1,0:T(8,128)(2,1)} %embed_ref.1) | copy-start | bytes 21676036
  17.5 2.3 %copy-start.1 = (bf16[1,6144,384]{2,1,0:T(8,128)(2,1)S(1)}, bf16[1,6144,384]{2,1,0:T(8,128)(2,1)}, u32[]{:S(2)}) copy-start(bf16[1,6144,384]{2,1,0:T(8,128)(2,1)} %param.21) | copy-start | bytes 14155780
  32.0 2.8 %copy-start.2 = (bf16[1,6144]{1,0:T(2,128)(2,1)S(1)}, bf16[1,6144]{1,0:T(2,128)(2,1)}, u32[]{:S(2)}) copy-start(bf16[1,6144]{1,0:T(2,128)(2,1)} %gain_ref.1) | copy-start | bytes 36868
  32.0 2.8 %copy-start.4 = (f32[1,2,128]{2,1,0:T(2,128)S(1)}, f32[1,2,128]{2,1,0:T(2,128)}, u32[]{:S(2)}) copy-start(f32[1,2,128]{2,1,0:T(2,128)} %param.22) | copy-start | bytes 3076
  33.4 17.2 %collective-permute-start.1 = (bf16[512,640]{1,0:T(8,128)(2,1)S(1)}, bf16[512,640]{1,0:T(8,128)(2,1)S(1)}, u32[]{:S(2)}, u32[]{:S(2)}) collective-permute-start(bf16[512,640]{1,0:T(8,128)(2,1)S(1)} %get-tuple-element.23.x_ref), channel_id=1, source_target_pairs={{0,1},{1,2},{2,3},{3,0},{4,5},{5,6},{6,7},{7,4},{8,9},{9,10},{10,1... | collective-permute-start | bytes 1966088 | tf_op jit(solution)/shard_map/ppermute | solution.py:386
  45.8 8.3 %collective-permute-start.3 = (bf16[64,6144]{1,0:T(8,128)(2,1)}, bf16[64,6144]{1,0:T(8,128)(2,1)S(1)}, u32[]{:S(2)}, u32[]{:S(2)}) collective-permute-start(bf16[64,6144]{1,0:T(8,128)(2,1)} %shard_map.122.half_hbm), channel_id=1, source_target_pairs={{0,4},{4,0},{8,12},{12,8},{16,20},{20,16},{24,28},{28,24},{32,36},... | collective-permute-start | bytes 2359304 | tf_op jit(solution)/shard_map/ppermute | solution.py:405
  48.1 6.0 %collective-permute-start.2 = (bf16[512,128]{1,0:T(8,128)(2,1)S(1)}, bf16[512,128]{1,0:T(8,128)(2,1)S(1)}, u32[]{:S(2)}, u32[]{:S(2)}) collective-permute-start(bf16[512,128]{1,0:T(8,128)(2,1)S(1)} %get-tuple-element.28), channel_id=1, source_target_pairs={{0,1},{1,2},{2,3},{3,0},{4,5},{5,6},{6,7},{7,4},{8,9},{9,10},{10,1... | collective-permute-start | bytes 393224 | tf_op jit(solution)/shard_map/ppermute | solution.py:401
